TPU v7x, 512 devices: a whole 4x4x16 slice. The times are simulated.
512 devices in a mesh: cuts: 32 (over z, x_lo), blk: 16 (over x_hi, y, core).
Axes of the slice: x: 4 (x_hi: 2, x_lo: 2; x = x_hi * 2 + x_lo), y: 4, z: 16, core: 2. Of those that a mesh axis runs over, the one named last changes fastest.
Arguments:
- steps: bfloat16 [512, 2, 512, 512], P(('cuts', 'blk')), as said below
Outputs:
- sidebands: float32 [32, 2, 512, 512], P(None, None, 'blk', 'cuts')
Inputs may be any that keep to these rules, and one draw needn't show every extreme that they name: `steps`: sqrt(512) times every entry lies between -1 and 1.
All inputs are finite; a program needn't handle non-finite values.
Results may differ from a plain program's by a relative error of at most 0.035.
Values may be sent and summed in bfloat16 or wider, within the bound.
A program may use at most 64 MiB of HBM per device.

v0:
```python
import math

import jax
import jax.numpy as jnp
from jax import lax
from jax.sharding import PartitionSpec as P


def from_partner(block, axis, distance):
    count = lax.axis_size(axis)
    route = []
    for low in range(count):
        high = low | 1 << distance
        if high != low and high < count:
            route += [(low, high), (high, low)]
    return lax.ppermute(block, axis, route)


def passed_along(x, axis, by):
    devices = lax.axis_size(axis)
    return lax.ppermute(x, axis, [(i, (i + by) % devices) for i in range(devices)])


def complex_product(left_factor, right_factor):
    real_real = jnp.dot(left_factor[0], right_factor[0], preferred_element_type=jnp.float32)
    imag_imag = jnp.dot(left_factor[1], right_factor[1], preferred_element_type=jnp.float32)
    real_imag = jnp.dot(left_factor[0], right_factor[1], preferred_element_type=jnp.float32)
    imag_real = jnp.dot(left_factor[1], right_factor[0], preferred_element_type=jnp.float32)
    return jnp.stack([real_real - imag_imag, real_imag + imag_real])


def complex_wide(left_factor, right_factor):
    hp = lax.Precision.HIGHEST
    real_real = jnp.dot(left_factor[0], right_factor[0], precision=hp)
    imag_imag = jnp.dot(left_factor[1], right_factor[1], precision=hp)
    real_imag = jnp.dot(left_factor[0], right_factor[1], precision=hp)
    imag_real = jnp.dot(left_factor[1], right_factor[0], precision=hp)
    return jnp.stack([real_real - imag_imag, real_imag + imag_real])


def group_product(left_factor, right_factor):
    if left_factor.dtype == jnp.bfloat16:
        return complex_product(left_factor, right_factor)
    return complex_wide(left_factor, right_factor)


def per_device(steps):
    current = steps[0]
    order = current.shape[-1]
    blk_count = lax.axis_size("blk")
    block_rows = order // blk_count
    tree_depth = blk_count.bit_length() - 1
    blk_index = lax.axis_index("blk")
    first_partner = from_partner(current, "blk", 0)
    for section in range(tree_depth):
        if section == 0:
            partner = first_partner
        else:
            partner = from_partner(current, "blk", section)
        is_upper = blk_index >> section & 1 == 1
        upper_factor = jnp.where(is_upper, current, partner)
        lower_factor = jnp.where(is_upper, partner, current)
        current = group_product(upper_factor, lower_factor)
    current = current.astype(jnp.bfloat16)
    row_block = lax.dynamic_slice_in_dim(current, blk_index * block_rows, block_rows, 1)
    cuts_count = lax.axis_size("cuts")
    loop_depth = cuts_count.bit_length() - 1
    for section in range(loop_depth):
        distance = 1 << section
        ahead = passed_along(row_block, "cuts", -distance)

        def add_rows(running, incoming, offset, ahead=ahead):
            return complex_product(ahead, incoming)

        empty_sum = jnp.zeros(row_block.shape, jnp.float32)
        running = add_rows(
            empty_sum, lax.all_gather(row_block, "blk", axis=1, tiled=True), jnp.int32(0)
        )
        row_block = running.astype(jnp.bfloat16)
    received = lax.all_to_all(row_block[None], "cuts", split_axis=3, concat_axis=0, tiled=True)
    slice_count = received.shape[0]
    freq_index = jnp.arange(slice_count, dtype=jnp.int32)
    phase_angle = (
        2.0
        * math.pi
        / slice_count
        * (freq_index[:, None] * freq_index[None, :] % slice_count).astype(jnp.float32)
    )
    cosine_table = jnp.cos(phase_angle)
    sine_table = jnp.sin(phase_angle)
    flattened = received.astype(jnp.float32).reshape(slice_count, 2, -1)
    hp = lax.Precision.HIGHEST
    real_part = jnp.dot(cosine_table, flattened[:, 0], precision=hp) + jnp.dot(
        sine_table, flattened[:, 1], precision=hp
    )
    imag_part = jnp.dot(cosine_table, flattened[:, 1], precision=hp) - jnp.dot(
        sine_table, flattened[:, 0], precision=hp
    )
    norm_factor = math.sqrt(order / slice_count)
    result = jnp.stack([real_part, imag_part], axis=1) * norm_factor
    return result.reshape(received.shape)


def solution(mesh):
    in_specs = (P(("cuts", "blk"), None, None, None),)
    out_specs = P(None, None, "blk", "cuts")
    return jax.shard_map(
        per_device, mesh=mesh, in_specs=in_specs, out_specs=out_specs, check_vma=False
    )
```

profile of v0, /device:TPU:1, one launch (start us, length us, event | category | flops | bytes accessed | tf_op | source)
XLA Modules:
  0.0 564.0 jit_solution(16650119582925848394)
XLA Ops:
  6.5 8.8 %collective-permute-start = (bf16[2,512,512]{2,1,0:T(8,128)(2,1)}, bf16[2,512,512]{2,1,0:T(8,128)(2,1)S(1)}, u32[]{:S(2)}, u32[]{:S(2)}) collective-permute-start(bf16[2,512,512]{2,1,0:T(8,128)(2,1)} %bitcast.207), channel_id=1, source_target_pairs={{0,1},{1,0},{2,3},{3,2},{4,5},{5,4},{6,7},{7,6},{8,9},{9,8},{10,11... | collective-permute-start | bytes 3145736 | tf_op jit(solution)/shard_map/ppermute | solution.py:16
  15.3 2.5 collective-permute-done
  17.8 1.4 broadcast_select_fusion.1
  20.9 1.5 pad_maximum_fusion
  22.4 1.9 collective-permute-start.1
  24.3 47.1 %collective-permute-done.1 = f32[2,512,512]{2,1,0:T(8,128)} collective-permute-done((f32[2,512,512]{2,1,0:T(8,128)}, f32[2,512,512]{2,1,0:T(8,128)}, u32[]{:S(2)}, u32[]{:S(2)}) %collective-permute-start.1) | collective-permute-done | bytes 2097184 | tf_op jit(solution)/shard_map/ppermute | solution.py:16
  71.5 2.3 broadcast_select_fusion.3
  73.8 1.8 fusion.31
  75.7 1.8 fusion.30
  77.5 1.9 fusion.3
  79.4 1.8 fusion.2
  81.2 1.5 pad_maximum_fusion.1
  82.7 2.1 collective-permute-start.2
  84.8 47.5 %collective-permute-done.2 = f32[2,512,512]{2,1,0:T(8,128)} collective-permute-done((f32[2,512,512]{2,1,0:T(8,128)}, f32[2,512,512]{2,1,0:T(8,128)}, u32[]{:S(2)}, u32[]{:S(2)}) %collective-permute-start.2) | collective-permute-done | bytes 2097184 | tf_op jit(solution)/shard_map/ppermute | solution.py:16
  132.4 2.3 broadcast_select_fusion.5
  134.7 1.8 fusion.33
  136.6 1.8 fusion.32
  138.4 1.8 fusion.1
  140.3 1.8 fusion
  142.1 1.5 pad_maximum_fusion.2
  143.6 2.1 collective-permute-start.3
  145.8 46.6 %collective-permute-done.3 = f32[2,512,512]{2,1,0:T(8,128)} collective-permute-done((f32[2,512,512]{2,1,0:T(8,128)}, f32[2,512,512]{2,1,0:T(8,128)}, u32[]{:S(2)}, u32[]{:S(2)}) %collective-permute-start.3) | collective-permute-done | bytes 2097184 | tf_op jit(solution)/shard_map/ppermute | solution.py:16
  192.3 2.3 broadcast_select_fusion.6
  194.7 1.9 fusion.34
  196.5 1.9 fusion.35
  198.4 1.9 fusion.8
  200.3 1.9 fusion.9
  202.9 6.7 %collective-permute-start.4 = (bf16[2,32,512]{2,1,0:T(8,128)(2,1)}, bf16[2,32,512]{2,1,0:T(8,128)(2,1)S(1)}, u32[]{:S(2)}, u32[]{:S(2)}) collective-permute-start(bf16[2,32,512]{2,1,0:T(8,128)(2,1)} %fusion.50), channel_id=1, source_target_pairs={{0,496},{16,0},{32,16},{48,32},{64,48},{80,64},{96,80},{112,96},{1... | collective-permute-start | bytes 196616 | tf_op jit(solution)/shard_map/ppermute | solution.py:21
  209.6 1.6 collective-permute-done.4
  211.2 53.9 %all-gather.6.cloned.1.call-done = bf16[2,512,512]{2,1,0:T(8,128)(2,1)} async-done(((bf16[2,32,512]{2,1,0:T(8,128)(2,1)}), bf16[2,512,512]{2,1,0:T(8,128)(2,1)}) %all-gather.6.cloned.1.call-update) | async-done | bytes 1048592 | tf_op jit(solution)/shard_map/all_gather | solution.py:77
  268.8 1.2 fusion.28
  270.7 5.7 %collective-permute-start.5 = (bf16[2,32,512]{2,1,0:T(8,128)(2,1)}, bf16[2,32,512]{2,1,0:T(8,128)(2,1)S(1)}, u32[]{:S(2)}, u32[]{:S(2)}) collective-permute-start(bf16[2,32,512]{2,1,0:T(8,128)(2,1)} %pad_maximum_fusion.3), channel_id=1, source_target_pairs={{0,480},{16,496},{32,0},{48,16},{64,32},{80,48},{96,64},{112,80},{... | collective-permute-start | bytes 196616 | tf_op jit(solution)/shard_map/ppermute | solution.py:21
  276.5 1.6 collective-permute-done.5
  278.1 51.8 %all-gather.8.cloned.1.call-done = bf16[2,512,512]{2,1,0:T(8,128)(2,1)} async-done(((bf16[2,32,512]{2,1,0:T(8,128)(2,1)}), bf16[2,512,512]{2,1,0:T(8,128)(2,1)}) %all-gather.8.cloned.1.call-update) | async-done | bytes 1048592 | tf_op jit(solution)/shard_map/all_gather | solution.py:77
  333.6 1.2 fusion.26
  335.5 6.5 %collective-permute-start.6 = (bf16[2,32,512]{2,1,0:T(8,128)(2,1)}, bf16[2,32,512]{2,1,0:T(8,128)(2,1)S(1)}, u32[]{:S(2)}, u32[]{:S(2)}) collective-permute-start(bf16[2,32,512]{2,1,0:T(8,128)(2,1)} %pad_maximum_fusion.4), channel_id=1, source_target_pairs={{0,448},{16,464},{32,480},{48,496},{64,0},{80,16},{96,32},{112,48}... | collective-permute-start | bytes 196616 | tf_op jit(solution)/shard_map/ppermute | solution.py:21
  342.1 3.1 collective-permute-done.6
  345.2 49.5 %all-gather.10.cloned.1.call-done = bf16[2,512,512]{2,1,0:T(8,128)(2,1)} async-done(((bf16[2,32,512]{2,1,0:T(8,128)(2,1)}), bf16[2,512,512]{2,1,0:T(8,128)(2,1)}) %all-gather.10.cloned.1.call-update) | async-done | bytes 1048592 | tf_op jit(solution)/shard_map/all_gather | solution.py:77
  397.1 1.2 fusion.25
  400.3 8.1 %collective-permute-start.7 = (bf16[2,32,512]{2,1,0:T(8,128)(2,1)}, bf16[2,32,512]{2,1,0:T(8,128)(2,1)S(1)}, u32[]{:S(2)}, u32[]{:S(2)}) collective-permute-start(bf16[2,32,512]{2,1,0:T(8,128)(2,1)} %pad_maximum_fusion.5), channel_id=1, source_target_pairs={{0,384},{16,400},{32,416},{48,432},{64,448},{80,464},{96,480},{112... | collective-permute-start | bytes 196616 | tf_op jit(solution)/shard_map/ppermute | solution.py:21
  408.4 6.1 %collective-permute-done.7 = bf16[2,32,512]{2,1,0:T(8,128)(2,1)S(1)} collective-permute-done((bf16[2,32,512]{2,1,0:T(8,128)(2,1)}, bf16[2,32,512]{2,1,0:T(8,128)(2,1)S(1)}, u32[]{:S(2)}, u32[]{:S(2)}) %collective-permute-start.7) | collective-permute-done | bytes 65568 | tf_op jit(solution)/shard_map/ppermute | solution.py:21
  414.6 44.9 %all-gather.12.cloned.1.call-done = bf16[2,512,512]{2,1,0:T(8,128)(2,1)} async-done(((bf16[2,32,512]{2,1,0:T(8,128)(2,1)}), bf16[2,512,512]{2,1,0:T(8,128)(2,1)}) %all-gather.12.cloned.1.call-update) | async-done | bytes 1048592 | tf_op jit(solution)/shard_map/all_gather | solution.py:77
  461.9 1.2 fusion.23
  465.1 12.5 %collective-permute-start.8 = (bf16[2,32,512]{2,1,0:T(8,128)(2,1)}, bf16[2,32,512]{2,1,0:T(8,128)(2,1)S(1)}, u32[]{:S(2)}, u32[]{:S(2)}) collective-permute-start(bf16[2,32,512]{2,1,0:T(8,128)(2,1)} %pad_maximum_fusion.6), channel_id=1, source_target_pairs={{0,256},{16,272},{32,288},{48,304},{64,320},{80,336},{96,352},{112... | collective-permute-start | bytes 196616 | tf_op jit(solution)/shard_map/ppermute | solution.py:21
  477.6 2.5 collective-permute-done.8
  480.1 44.1 %all-gather.14.cloned.1.call-done = bf16[2,512,512]{2,1,0:T(8,128)(2,1)} async-done(((bf16[2,32,512]{2,1,0:T(8,128)(2,1)}), bf16[2,512,512]{2,1,0:T(8,128)(2,1)}) %all-gather.14.cloned.1.call-update) | async-done | bytes 1048592 | tf_op jit(solution)/shard_map/all_gather | solution.py:77
  529.6 24.7 %all_to_all.15 = bf16[32,2,512]{2,1,0:T(2,128)(2,1)S(1)} all-to-all(bf16[32,2,512]{2,1,0:T(2,128)(2,1)S(1)} %reshape.43), channel_id=1, replica_groups=mesh['cuts'=32,'blk'=16] {'cuts'}, dimensions={0} | all-to-all | bytes 131072 | tf_op jit(solution)/shard_map/all_to_all | solution.py:80
  556.2 1.3 copy.18
  (48 shorter events, 27.3 us)
Async XLA Ops:
  6.5 258.5 %all-gather.6.cloned.1.call-start = ((), (), s32[]{:S(2)}) async-start(), calls=%async_computation.1 | async-start | bytes 1114112 | tf_op jit(solution)/shard_map/all_gather | solution.py:77
  6.5 11.3 %collective-permute-start = (bf16[2,512,512]{2,1,0:T(8,128)(2,1)}, bf16[2,512,512]{2,1,0:T(8,128)(2,1)S(1)}, u32[]{:S(2)}, u32[]{:S(2)}) collective-permute-start(bf16[2,512,512]{2,1,0:T(8,128)(2,1)} %bitcast.207), channel_id=1, source_target_pairs={{0,1},{1,0},{2,3},{3,2},{4,5},{5,4},{6,7},{7,6},{8,9},{9,8},{10,11... | collective-permute-start | bytes 3145736 | tf_op jit(solution)/shard_map/ppermute | solution.py:16
  22.4 49.0 %collective-permute-start.1 = (f32[2,512,512]{2,1,0:T(8,128)}, f32[2,512,512]{2,1,0:T(8,128)}, u32[]{:S(2)}, u32[]{:S(2)}) collective-permute-start(f32[2,512,512]{2,1,0:T(8,128)} %pad_maximum_fusion), channel_id=1, source_target_pairs={{0,2},{2,0},{1,3},{3,1},{4,6},{6,4},{5,7},{7,5},{8,10},{10,8},{9,1... | collective-permute-start | bytes 6291464 | tf_op jit(solution)/shard_map/ppermute | solution.py:16
  82.7 49.6 %collective-permute-start.2 = (f32[2,512,512]{2,1,0:T(8,128)}, f32[2,512,512]{2,1,0:T(8,128)}, u32[]{:S(2)}, u32[]{:S(2)}) collective-permute-start(f32[2,512,512]{2,1,0:T(8,128)} %pad_maximum_fusion.1), channel_id=1, source_target_pairs={{0,4},{4,0},{1,5},{5,1},{2,6},{6,2},{3,7},{7,3},{8,12},{12,8},{9,1... | collective-permute-start | bytes 6291464 | tf_op jit(solution)/shard_map/ppermute | solution.py:16
  143.6 48.7 %collective-permute-start.3 = (f32[2,512,512]{2,1,0:T(8,128)}, f32[2,512,512]{2,1,0:T(8,128)}, u32[]{:S(2)}, u32[]{:S(2)}) collective-permute-start(f32[2,512,512]{2,1,0:T(8,128)} %pad_maximum_fusion.2), channel_id=1, source_target_pairs={{0,8},{8,0},{1,9},{9,1},{2,10},{10,2},{3,11},{11,3},{4,12},{12,4},... | collective-permute-start | bytes 6291464 | tf_op jit(solution)/shard_map/ppermute | solution.py:16
  202.8 127.0 %all-gather.8.cloned.1.call-start = ((), (), s32[]{:S(2)}) async-start(), calls=%async_computation.2 | async-start | bytes 1114112 | tf_op jit(solution)/shard_map/all_gather | solution.py:77
  202.9 8.3 %collective-permute-start.4 = (bf16[2,32,512]{2,1,0:T(8,128)(2,1)}, bf16[2,32,512]{2,1,0:T(8,128)(2,1)S(1)}, u32[]{:S(2)}, u32[]{:S(2)}) collective-permute-start(bf16[2,32,512]{2,1,0:T(8,128)(2,1)} %fusion.50), channel_id=1, source_target_pairs={{0,496},{16,0},{32,16},{48,32},{64,48},{80,64},{96,80},{112,96},{1... | collective-permute-start | bytes 196616 | tf_op jit(solution)/shard_map/ppermute | solution.py:21
  270.7 123.9 %all-gather.10.cloned.1.call-start = ((), (), s32[]{:S(2)}) async-start(), calls=%async_computation.3 | async-start | bytes 1114112 | tf_op jit(solution)/shard_map/all_gather | solution.py:77
  270.7 7.3 %collective-permute-start.5 = (bf16[2,32,512]{2,1,0:T(8,128)(2,1)}, bf16[2,32,512]{2,1,0:T(8,128)(2,1)S(1)}, u32[]{:S(2)}, u32[]{:S(2)}) collective-permute-start(bf16[2,32,512]{2,1,0:T(8,128)(2,1)} %pad_maximum_fusion.3), channel_id=1, source_target_pairs={{0,480},{16,496},{32,0},{48,16},{64,32},{80,48},{96,64},{112,80},{... | collective-permute-start | bytes 196616 | tf_op jit(solution)/shard_map/ppermute | solution.py:21
  335.5 123.9 %all-gather.12.cloned.1.call-start = ((), (), s32[]{:S(2)}) async-start(), calls=%async_computation.4 | async-start | bytes 1114112 | tf_op jit(solution)/shard_map/all_gather | solution.py:77
  335.5 9.6 %collective-permute-start.6 = (bf16[2,32,512]{2,1,0:T(8,128)(2,1)}, bf16[2,32,512]{2,1,0:T(8,128)(2,1)S(1)}, u32[]{:S(2)}, u32[]{:S(2)}) collective-permute-start(bf16[2,32,512]{2,1,0:T(8,128)(2,1)} %pad_maximum_fusion.4), channel_id=1, source_target_pairs={{0,448},{16,464},{32,480},{48,496},{64,0},{80,16},{96,32},{112,48}... | collective-permute-start | bytes 196616 | tf_op jit(solution)/shard_map/ppermute | solution.py:21
  400.3 123.9 %all-gather.14.cloned.1.call-start = ((), (), s32[]{:S(2)}) async-start(), calls=%async_computation.5 | async-start | bytes 1114112 | tf_op jit(solution)/shard_map/all_gather | solution.py:77
  400.3 14.2 %collective-permute-start.7 = (bf16[2,32,512]{2,1,0:T(8,128)(2,1)}, bf16[2,32,512]{2,1,0:T(8,128)(2,1)S(1)}, u32[]{:S(2)}, u32[]{:S(2)}) collective-permute-start(bf16[2,32,512]{2,1,0:T(8,128)(2,1)} %pad_maximum_fusion.5), channel_id=1, source_target_pairs={{0,384},{16,400},{32,416},{48,432},{64,448},{80,464},{96,480},{112... | collective-permute-start | bytes 196616 | tf_op jit(solution)/shard_map/ppermute | solution.py:21
  465.1 15.0 %collective-permute-start.8 = (bf16[2,32,512]{2,1,0:T(8,128)(2,1)}, bf16[2,32,512]{2,1,0:T(8,128)(2,1)S(1)}, u32[]{:S(2)}, u32[]{:S(2)}) collective-permute-start(bf16[2,32,512]{2,1,0:T(8,128)(2,1)} %pad_maximum_fusion.6), channel_id=1, source_target_pairs={{0,256},{16,272},{32,288},{48,304},{64,320},{80,336},{96,352},{112... | collective-permute-start | bytes 196616 | tf_op jit(solution)/shard_map/ppermute | solution.py:21
Sparse Core Ops, SparseCore 0:
  203.0 62.0 all-gather.5
  270.8 58.9 all-gather.7
  335.6 58.9 all-gather.9
  400.4 58.9 all-gather.11
  465.2 58.9 all-gather.13
where the time goes:
time: 566 us; the launch traced here: 564 us
  waiting for transfers between devices  403 us (71%)
  starting transfers between devices  54.6 us (10%)
  matrix products  49.7 us (9%)
  blocking collectives  24.7 us (4%)
  other arithmetic  16.2 us (3%)
  between operations  13.5 us (2%)
    all_gather x5, waiting for transfers between devices, per_device(): lax.all_gather(row_block, 'blk', axis=1, tiled=True)  244 us
    ppermute x4, waiting for transfers between devices, from_partner(): return lax.ppermute(block, axis, route)  144 us
    ppermute x5, starting transfers between devices, passed_along(): lax.ppermute(x, axis, [(i, (i + by) % devices) for i in range(devices)])  39.6 us
    all_to_all x1, blocking collectives, per_device(): lax.all_to_all(row_block[None], 'cuts', split_axis=3, concat_axis=0, tile...  24.7 us
    ppermute x5, waiting for transfers between devices, passed_along(): lax.ppermute(x, axis, [(i, (i + by) % devices) for i in range(devices)])  15 us
    ppermute x4, starting transfers between devices, from_partner(): return lax.ppermute(block, axis, route)  14.9 us
  transfers between devices with their start and end apart: 14, of which 14 were waited for; matrix products, arithmetic and copies ran while one was open for 0% of the time, Pallas kernels for 0%

commit v1 on v0

v1 whole, which is shorter than its diff:
```python
import math

import jax
import jax.numpy as jnp
from jax import lax
from jax.experimental import pallas as pl
from jax.experimental.pallas import tpu as pltpu
from jax.sharding import PartitionSpec as P

MESH = pl.DeviceIdType.MESH
F32 = jnp.float32
BF16 = jnp.bfloat16
LEVELS = 5


def dot(a, b):
    return jnp.dot(a, b, preferred_element_type=F32)


def arrived(ref, sem):
    pltpu.make_async_copy(ref, ref, sem).wait()


def send(src, dst, send_sem, recv_sem, device):
    pltpu.make_async_remote_copy(
        src_ref=src,
        dst_ref=dst,
        send_sem=send_sem,
        recv_sem=recv_sem,
        device_id=device,
        device_id_type=MESH,
    ).start()


def combine(by_real, by_imag):
    rows = by_real.shape[0] // 2
    return by_real[:rows] - by_imag[rows:], by_imag[:rows] + by_real[rows:]


def halves(value):
    high = value.astype(BF16)
    return high, (value - high.astype(F32)).astype(BF16)


def kernel(
    x_ref, o_ref,
    left, right, pairs, pair_low, chain, acc, ends, sibling, shifted, gathered, period, tiles, landed,
    left_sem, right_sem, left_out, right_out, pair_sem, pair_out, chain_sem, chain_out,
    ends_sem, ends_out, sib_sem, sib_out, shift_sem, shift_out, gather_sem, gather_out, all_sem, all_out,
):
    c = lax.axis_index("cuts")
    b = lax.axis_index("blk")
    xh = lax.div(b, 8)
    y = lax.rem(lax.div(b, 2), 4)
    h = lax.rem(b, 2)
    other = 1 - h
    sib = (c, b + 1 - 2 * h)
    opposite = (c, b + 8 - 16 * xh)

    def along_y(d):
        return (c, xh * 8 + lax.rem(y + d, 4) * 2 + h)

    def cut(k):
        return (lax.rem(c + k + 32, 32), b)

    @pl.when(h == 0)
    def _():
        pltpu.make_async_copy(x_ref.at[0, :, :, pl.ds(0, 256)], right, right_sem).start()

    @pl.when(h == 1)
    def _():
        for r in range(4):
            for q in range(2):
                pltpu.make_async_copy(
                    x_ref.at[0, :, pl.ds(128 * r, 128), pl.ds(256 * q, 256)],
                    left.at[q, :, pl.ds(128 * r, 128)],
                    left_sem.at[r, q],
                ).start()

    barrier = pltpu.get_barrier_semaphore()
    greet = [sib, opposite] + [along_y(d) for d in (1, 2, 3)] + [cut(1 << s) for s in range(LEVELS)]
    for device in greet:
        pl.semaphore_signal(barrier, inc=1, device_id=device, device_id_type=MESH)
    pl.semaphore_wait(barrier, len(greet))

    @pl.when(h == 0)
    def _():
        send(x_ref.at[0, :, :, pl.ds(256, 256)], right, right_out, right_sem, sib)

    @pl.when(h == 1)
    def _():
        for r in range(4):
            for q in range(2):
                send(
                    x_ref.at[0, :, pl.ds(128 * r, 128), pl.ds(256 * q, 256)],
                    left.at[q, :, pl.ds(128 * r, 128)],
                    left_out.at[r, q],
                    left_sem.at[r, q],
                    sib,
                )

    arrived(right, right_sem)

    def pair_chunk(r, carry):
        rows = pl.ds(pl.multiple_of(128 * r, 128), 128)
        for q in range(2):
            arrived(left.at[q, :, rows], left_sem.at[r, q])
        x0 = left[0, :, rows, :].reshape(256, 256)
        x1 = left[1, :, rows, :].reshape(256, 256)
        by = [dot(x0, right[i, :256]) + dot(x1, right[i, 256:]) for i in range(2)]
        for i, part in enumerate(combine(*by)):
            high, low = halves(part)
            pairs[y, i, rows, :] = high
            pair_low[i, rows, :] = low
        for d in (1, 3, 2):
            block = pairs.at[y, :, rows]
            send(block, block, pair_out.at[d - 1, r], pair_sem.at[d - 1, r], along_y(d))
        return carry

    lax.fori_loop(0, 4, pair_chunk, 0)

    def wait_pair(j):
        @pl.when(y != j)
        def _():
            d = lax.rem(y - j + 4, 4)
            for r in range(4):
                arrived(pairs.at[j, :, pl.ds(128 * r, 128)], pair_sem.at[d - 1, r])

    def exchange_chain(s):
        send(chain.at[s, h], chain.at[s, h], chain_out.at[s], chain_sem.at[s], sib)

    wait_pair(3)
    for i in range(2):
        for p in range(2):
            rows = pl.ds(pl.multiple_of(256 * p + 64 * y, 64), 64)
            chain[0, h, 0, i, p] = pairs[3, i, rows, :]
            low = pair_low[i, rows, :]
            chain[0, h, 1, i, p] = jnp.where(y == 3, low, jnp.zeros_like(low))
    exchange_chain(0)
    for s in range(3):
        j = 2 - s
        wait_pair(j)
        arrived(chain.at[s, other], chain_sem.at[s])
        x0 = chain[s, 0].reshape(512, 256)
        x1 = chain[s, 1].reshape(512, 256)
        for i in range(2):
            t = dot(x0, pairs[j, i, :256]) + dot(x1, pairs[j, i, 256:])
            acc[i] = t[:256] + t[256:]

        @pl.when(y == j)
        def _():
            for i in range(2):
                acc[i] += dot(x0[:256], pair_low[i, :256]) + dot(x1[:256], pair_low[i, 256:])

        for i, part in enumerate(combine(acc[0], acc[1])):
            part = part.reshape(2, 64, 256)
            if s < 2:
                chain[s + 1, h, 0, i], chain[s + 1, h, 1, i] = halves(part)
            else:
                ends[xh, i] = part.astype(BF16)
        if s < 2:
            exchange_chain(s + 1)

    def spread(src, level):
        for d in (1, 3, 2):
            send(
                src, gathered.at[level, :, :, y],
                gather_out.at[level, d - 1], gather_sem.at[level, d - 1], along_y(d),
            )

    def product(own, level):
        for d in (1, 2, 3):
            arrived(gathered.at[level, :, :, lax.rem(y - d + 4, 4)], gather_sem.at[level, d - 1])
        x0 = own[...].reshape(256, 256)
        by = [dot(x0, gathered[level, i, h].reshape(256, 256)) for i in range(2)]
        arrived(sibling.at[level], sib_sem.at[level])
        x1 = sibling[level].reshape(256, 256)
        by = [by[i] + dot(x1, gathered[level, i, other].reshape(256, 256)) for i in range(2)]
        for i, part in enumerate(combine(*by)):
            part = part.reshape(2, 64, 256).astype(BF16)
            period[level, i] = part
            gathered[level + 1, i, :, y] = part

    send(ends.at[xh], ends.at[xh], ends_out, ends_sem, opposite)
    arrived(ends.at[1 - xh], ends_sem)
    spread(ends.at[0], 0)
    send(ends.at[1], sibling.at[0], sib_out.at[0], sib_sem.at[0], sib)
    gathered[0, :, :, y] = ends[0]
    product(ends.at[1], 0)

    def double(level, k):
        send(period.at[level], shifted.at[level], shift_out.at[level], shift_sem.at[level], cut(-k))
        spread(period.at[level], level + 1)
        arrived(shifted.at[level], shift_sem.at[level])
        send(shifted.at[level], sibling.at[level + 1], sib_out.at[level + 1], sib_sem.at[level + 1], sib)
        product(shifted.at[level], level + 1)
        return 2 * k

    lax.fori_loop(0, LEVELS, double, jnp.int32(1))

    final = period[LEVELS, :, xh].astype(F32)
    stacked = jnp.concatenate([final[0, :32], final[1, :32], final[0, 32:], final[1, 32:]], axis=0)
    turned = stacked.T
    tiles[0] = turned.astype(BF16).reshape(16, 16, 128)
    turned = jnp.concatenate([turned[:, 64:], turned[:, :64]], axis=1)
    tiles[1] = turned.astype(BF16).reshape(16, 16, 128)

    def scatter(j, carry):
        target = 16 * h + j
        for core in range(2):
            here = (target == c) & (h == core)

            @pl.when(here)
            def _():
                pltpu.make_async_copy(tiles.at[core, j], landed.at[c], all_sem).start()

            @pl.when(jnp.logical_not(here))
            def _():
                send(
                    tiles.at[core, j], landed.at[c], all_out.at[core, j], all_sem,
                    (target, xh * 8 + y * 2 + core),
                )
        return carry

    lax.fori_loop(0, 16, scatter, 0)

    @pl.when(h == 0)
    def _():
        arrived(right, right_out)

    @pl.when(h == 1)
    def _():
        for r in range(4):
            for q in range(2):
                arrived(left.at[q, :, pl.ds(128 * r, 128)], left_out.at[r, q])

    for d in range(3):
        for r in range(4):
            arrived(pairs.at[y, :, pl.ds(128 * r, 128)], pair_out.at[d, r])
    for s in range(3):
        arrived(chain.at[s, h], chain_out.at[s])
    arrived(ends.at[xh], ends_out)

    def level_sent(level, carry):
        for d in range(3):
            arrived(gathered.at[level, :, :, y], gather_out.at[level, d])
        arrived(sibling.at[level], sib_out.at[level])
        return carry

    lax.fori_loop(0, LEVELS + 1, level_sent, 0)

    def shift_sent(level, carry):
        arrived(period.at[level], shift_out.at[level])
        return carry

    lax.fori_loop(0, LEVELS, shift_sent, 0)

    def scatter_sent(j, carry):
        for core in range(2):
            @pl.when(jnp.logical_not((16 * h + j == c) & (h == core)))
            def _():
                arrived(tiles.at[core, j], all_out.at[core, j])
        return carry

    lax.fori_loop(0, 16, scatter_sent, 0)
    arrived(landed, all_sem)
    o_ref[...] = landed[...]


def per_device(steps):
    dma = pltpu.SemaphoreType.DMA
    landed = pl.pallas_call(
        kernel,
        out_shape=jax.ShapeDtypeStruct((32, 16, 128), BF16),
        in_specs=[pl.BlockSpec(memory_space=pl.ANY)],
        out_specs=pl.BlockSpec(memory_space=pltpu.VMEM),
        scratch_shapes=[
            pltpu.VMEM((2, 2, 512, 256), BF16),
            pltpu.VMEM((2, 512, 256), BF16),
            pltpu.VMEM((4, 2, 512, 256), BF16),
            pltpu.VMEM((2, 512, 256), BF16),
            pltpu.VMEM((3, 2, 2, 2, 2, 64, 256), BF16),
            pltpu.VMEM((2, 256, 256), F32),
            pltpu.VMEM((2, 2, 2, 64, 256), BF16),
            pltpu.VMEM((LEVELS + 1, 2, 2, 64, 256), BF16),
            pltpu.VMEM((LEVELS, 2, 2, 64, 256), BF16),
            pltpu.VMEM((LEVELS + 2, 2, 2, 4, 64, 256), BF16),
            pltpu.VMEM((LEVELS + 1, 2, 2, 64, 256), BF16),
            pltpu.VMEM((2, 16, 16, 128), BF16),
            pltpu.VMEM((32, 16, 128), BF16),
            dma((4, 2)), dma, dma((4, 2)), dma,
            dma((3, 4)), dma((3, 4)), dma((3,)), dma((3,)),
            dma, dma, dma((LEVELS + 1,)), dma((LEVELS + 1,)),
            dma((LEVELS,)), dma((LEVELS,)), dma((LEVELS + 1, 3)), dma((LEVELS + 1, 3)),
            dma, dma((2, 16)),
        ],
        compiler_params=pltpu.CompilerParams(
            collective_id=0, has_side_effects=True, vmem_limit_bytes=40 * 1024 * 1024
        ),
        cost_estimate=pl.CostEstimate(
            flops=8 * 512 * 512 * 512 * 3, bytes_accessed=4 * 1024 * 1024, transcendentals=0
        ),
        name="propagate",
    )(steps)
    count = 32
    index = jnp.arange(count, dtype=jnp.int32)
    angle = 2.0 * math.pi / count * (index[:, None] * index[None, :] % count).astype(F32)
    cosine, sine = jnp.cos(angle), jnp.sin(angle)
    values = landed.astype(F32)
    real_in = values[:, :, :32].reshape(count, 512)
    imag_in = values[:, :, 32:64].reshape(count, 512)
    hp = lax.Precision.HIGHEST
    real = jnp.dot(cosine, real_in, precision=hp) + jnp.dot(sine, imag_in, precision=hp)
    imag = jnp.dot(cosine, imag_in, precision=hp) - jnp.dot(sine, real_in, precision=hp)
    result = jnp.stack([real, imag], axis=1) * math.sqrt(512 / count)
    return result.reshape(count, 2, 16, 32).transpose(0, 1, 3, 2)


def solution(mesh):
    return jax.shard_map(
        per_device,
        mesh=mesh,
        in_specs=(P(("cuts", "blk"), None, None, None),),
        out_specs=P(None, None, "blk", "cuts"),
        check_vma=False,
    )
```

time: 566 us -> 138 us (0.24)
  waiting for transfers between devices: 403 us -> 0 us
  Pallas kernels: 0 us -> 134 us
  starting transfers between devices: 54.6 us -> 0 us
  matrix products: 49.7 us -> 0.94 us
  blocking collectives: 24.7 us -> 0 us
  other arithmetic: 16.2 us -> 0.87 us
  between operations: 13.5 us -> 0.03 us
    all_gather x5 -> x0, waiting for transfers between devices: 244 us -> none  [per_device(): lax.all_gather(row_block, 'blk', axis=1, tiled=True)]
    ppermute x9 -> x0, waiting for transfers between devices: 159 us -> none  [the longest x4 144 us: from_partner(): return lax.ppermute(block, axis, route)]
    pallas_call x0 -> x1, Pallas kernels: none -> 134 us  [per_device(): pl.pallas_call(kernel, out_shape=jax.ShapeDtypeStruct((32, 16, 128), BF16...]
    ppermute x9 -> x0, starting transfers between devices: 54.5 us -> none  [the longest x5 39.6 us: passed_along(): lax.ppermute(x, axis, [(i, (i + by) % devices) for i in range(devices)])]
    dot_general x40 -> x4, matrix products: 49.7 us -> 0.94 us  [the longest x1 0.24 us: per_device(): jnp.dot(cosine, imag_in, precision=hp)]
    all_to_all x1 -> x0, blocking collectives: 24.7 us -> none  [per_device(): lax.all_to_all(row_block[None], 'cuts', split_axis=3, concat_axis=0, tile...]
    select_n x4 -> x0, other arithmetic: 8.35 us -> none  [the longest x3 6.02 us: per_device(): upper_factor = jnp.where(is_upper, current, partner)]
    another operation x9 -> x0, other arithmetic: 7.78 us -> none  [the longest x6 4.14 us: complex_product(): return jnp.stack([real_real - imag_imag, real_imag + imag_real])]
  transfers between devices with their start and end apart: 14 -> 0, of which waited for: 14 -> 0; matrix products, arithmetic and copies ran while one was open for 0% -> 0% of each run, Pallas kernels for 0% -> 0%
where the time goes in v1:
time: 138 us; the launch traced here: 137 us
  Pallas kernels  134 us (97%)
  local copies, waits for them, and re-layouts  1.87 us (1%)
    pallas_call x1, Pallas kernels, per_device(): pl.pallas_call(kernel, out_shape=jax.ShapeDtypeStruct((32, 16, 128), BF16...  134 us

profile of v1, /device:TPU:1, one launch (start us, length us, event | category | flops | bytes accessed | tf_op | source)
XLA Modules:
  0.0 137.4 jit_solution(2278408609750361479)
XLA Ops:
  0.0 0.0 copy-start
  0.0 1.2 copy-done
  1.2 133.6 %propagate.1 = bf16[32,16,128]{2,1,0:T(8,128)(2,1)S(1)} custom-call(bf16[1,2,512,512]{3,2,1,0:T(8,128)(2,1)S(1)} %copy-done), custom_call_target="tpu_custom_call" | custom-call | flops 3221225472 | bytes 4194304 | tf_op jit(solution)/shard_map/propagate/pallas_call | solution.py:272
  134.9 0.1 fusion.31
  135.0 0.2 reshape.11
  135.2 0.2 reshape.12
  135.3 0.2 fusion.9
  135.5 0.2 convolution_subtract_fusion
  135.8 0.2 fusion.11
  136.0 0.2 convolution_add_fusion
  136.3 0.1 stack.9
  136.4 0.1 stack.10
  136.5 0.9 fusion
Async XLA Ops:
  0.0 1.2 copy-start

commit v2 on v1

--- a/solution.py
+++ b/solution.py
@@ -11,6 +11,7 @@
 F32 = jnp.float32
 BF16 = jnp.bfloat16
 LEVELS = 5
+WIDE = 3
 
 
 def dot(a, b):
@@ -44,9 +45,11 @@
 
 def kernel(
     x_ref, o_ref,
-    left, right, pairs, pair_low, chain, acc, ends, sibling, shifted, gathered, period, tiles, landed,
+    left, right, pairs, pair_low, chain, acc, ends, sibling, shifted, gathered, period,
+    late_shift, late_sib, late, tiles, landed,
     left_sem, right_sem, left_out, right_out, pair_sem, pair_out, chain_sem, chain_out,
-    ends_sem, ends_out, sib_sem, sib_out, shift_sem, shift_out, gather_sem, gather_out, all_sem, all_out,
+    ends_sem, ends_out, sib_sem, sib_out, shift_sem, shift_out, gather_sem, gather_out,
+    late_sem, late_out, all_sem, all_out,
 ):
     c = lax.axis_index("cuts")
     b = lax.axis_index("blk")
@@ -161,51 +164,91 @@
         if s < 2:
             exchange_chain(s + 1)
 
-    def spread(src, level):
+    def spread(src, level, order, p):
         for d in (1, 3, 2):
             send(
-                src, gathered.at[level, :, :, y],
-                gather_out.at[level, d - 1], gather_sem.at[level, d - 1], along_y(d),
+                src, gathered.at[level, :, p, y],
+                gather_out.at[level, order, d - 1], gather_sem.at[level, order, d - 1], along_y(d),
             )
 
-    def product(own, level):
+    def spread_arrived(level, order, p):
         for d in (1, 2, 3):
-            arrived(gathered.at[level, :, :, lax.rem(y - d + 4, 4)], gather_sem.at[level, d - 1])
-        x0 = own[...].reshape(256, 256)
-        by = [dot(x0, gathered[level, i, h].reshape(256, 256)) for i in range(2)]
-        arrived(sibling.at[level], sib_sem.at[level])
-        x1 = sibling[level].reshape(256, 256)
-        by = [by[i] + dot(x1, gathered[level, i, other].reshape(256, 256)) for i in range(2)]
-        for i, part in enumerate(combine(*by)):
+            arrived(gathered.at[level, :, p, lax.rem(y - d + 4, 4)], gather_sem.at[level, order, d - 1])
+
+    def half_product(x, level, p):
+        return [dot(x, gathered[level, i, p].reshape(256, 256)) for i in range(2)]
+
+    def product(own, theirs, theirs_sem, level):
+        rows = 2 * math.prod(own.shape[1:-1])
+        spread_arrived(level, 0, h)
+        by = half_product(own[...].reshape(rows, 256), level, h)
+        arrived(theirs, theirs_sem)
+        spread_arrived(level, 1, other)
+        more = half_product(theirs[...].reshape(rows, 256), level, other)
+        return combine(by[0] + more[0], by[1] + more[1])
+
+    def keep(parts, level):
+        for i, part in enumerate(parts):
             part = part.reshape(2, 64, 256).astype(BF16)
             period[level, i] = part
             gathered[level + 1, i, :, y] = part
 
-    send(ends.at[xh], ends.at[xh], ends_out, ends_sem, opposite)
-    arrived(ends.at[1 - xh], ends_sem)
-    spread(ends.at[0], 0)
+    for order, p in enumerate((h, other)):
+        send(ends.at[xh, :, p], ends.at[xh, :, p], ends_out.at[order], ends_sem.at[order], opposite)
+    for order, p in enumerate((h, other)):
+        arrived(ends.at[1 - xh, :, p], ends_sem.at[order])
+        spread(ends.at[0, :, p], 0, order, p)
     send(ends.at[1], sibling.at[0], sib_out.at[0], sib_sem.at[0], sib)
     gathered[0, :, :, y] = ends[0]
-    product(ends.at[1], 0)
+    keep(product(ends.at[1], sibling.at[0], sib_sem.at[0], 0), 0)
 
     def double(level, k):
         send(period.at[level], shifted.at[level], shift_out.at[level], shift_sem.at[level], cut(-k))
-        spread(period.at[level], level + 1)
+        for order, p in enumerate((h, other)):
+            spread(period.at[level, :, p], level + 1, order, p)
         arrived(shifted.at[level], shift_sem.at[level])
-        send(shifted.at[level], sibling.at[level + 1], sib_out.at[level + 1], sib_sem.at[level + 1], sib)
-        product(shifted.at[level], level + 1)
+        after = level + 1
+        send(shifted.at[level], sibling.at[after], sib_out.at[after], sib_sem.at[after], sib)
+        keep(product(shifted.at[level], sibling.at[after], sib_sem.at[after], after), after)
         return 2 * k
 
-    lax.fori_loop(0, LEVELS, double, jnp.int32(1))
-
-    final = period[LEVELS, :, xh].astype(F32)
-    stacked = jnp.concatenate([final[0, :32], final[1, :32], final[0, 32:], final[1, 32:]], axis=0)
+    lax.fori_loop(0, WIDE, double, jnp.int32(1))
+
+    send(period.at[WIDE, :, xh], late_shift.at[0], late_out.at[0], late_sem.at[0], cut(-8))
+    for order, p in enumerate((h, other)):
+        spread(period.at[WIDE, :, p], WIDE + 1, order, p)
+    arrived(late_shift.at[0], late_sem.at[0])
+    send(late_shift.at[0], late_sib.at[0], late_out.at[1], late_sem.at[1], sib)
+    for i, part in enumerate(product(late_shift.at[0], late_sib.at[0], late_sem.at[1], WIDE + 1)):
+        part = part.astype(BF16)
+        late[0, i] = part
+        gathered[WIDE + 2, i, xh, y] = part
+
+    send(late.at[0], late_shift.at[1], late_out.at[2], late_sem.at[2], cut(-16))
+    send(late.at[0], late.at[1], late_out.at[3], late_sem.at[3], opposite)
+    level = WIDE + 2
+    spread(late.at[0], level, lax.rem(xh + h, 2), xh)
+    arrived(late.at[1], late_sem.at[3])
+    spread(late.at[1], level, lax.rem(1 - xh + h, 2), 1 - xh)
+    gathered[level, :, 1 - xh, y] = late[1]
+    arrived(late_shift.at[1], late_sem.at[2])
+    send(late_shift.at[1], late_sib.at[1], late_out.at[4], late_sem.at[4], sib)
+    real, imag = product(late_shift.at[1], late_sib.at[1], late_sem.at[4], level)
+
+    stacked = jnp.concatenate([real[:32], imag[:32], real[32:], imag[32:]], axis=0)
     turned = stacked.T
     tiles[0] = turned.astype(BF16).reshape(16, 16, 128)
     turned = jnp.concatenate([turned[:, 64:], turned[:, :64]], axis=1)
     tiles[1] = turned.astype(BF16).reshape(16, 16, 128)
-
-    def scatter(j, carry):
+    same = lax.div(c, 16) == h
+
+    def nearness(t):
+        t = jnp.where(same, 15 - t, t)
+        step = lax.div(t + 1, 2)
+        return lax.rem(c + jnp.where(lax.rem(t, 2) == 1, step, 16 - step), 16)
+
+    def scatter(t, carry):
+        j = nearness(t)
         target = 16 * h + j
         for core in range(2):
             here = (target == c) & (h == core)
@@ -239,21 +282,30 @@
             arrived(pairs.at[y, :, pl.ds(128 * r, 128)], pair_out.at[d, r])
     for s in range(3):
         arrived(chain.at[s, h], chain_out.at[s])
-    arrived(ends.at[xh], ends_out)
+    for order in range(2):
+        arrived(ends.at[xh, :, 0], ends_out.at[order])
 
     def level_sent(level, carry):
-        for d in range(3):
-            arrived(gathered.at[level, :, :, y], gather_out.at[level, d])
-        arrived(sibling.at[level], sib_out.at[level])
-        return carry
-
-    lax.fori_loop(0, LEVELS + 1, level_sent, 0)
+        for order in range(2):
+            for d in range(3):
+                arrived(gathered.at[level, :, 0, y], gather_out.at[level, order, d])
+        return carry
+
+    lax.fori_loop(0, WIDE + 3, level_sent, 0)
 
     def shift_sent(level, carry):
         arrived(period.at[level], shift_out.at[level])
         return carry
 
-    lax.fori_loop(0, LEVELS, shift_sent, 0)
+    lax.fori_loop(0, WIDE, shift_sent, 0)
+
+    def sibling_sent(level, carry):
+        arrived(sibling.at[level], sib_out.at[level])
+        return carry
+
+    lax.fori_loop(0, WIDE + 1, sibling_sent, 0)
+    for n in range(5):
+        arrived(late.at[0], late_out.at[n])
 
     def scatter_sent(j, carry):
         for core in range(2):
@@ -282,20 +334,23 @@
             pltpu.VMEM((3, 2, 2, 2, 2, 64, 256), BF16),
             pltpu.VMEM((2, 256, 256), F32),
             pltpu.VMEM((2, 2, 2, 64, 256), BF16),
-            pltpu.VMEM((LEVELS + 1, 2, 2, 64, 256), BF16),
-            pltpu.VMEM((LEVELS, 2, 2, 64, 256), BF16),
-            pltpu.VMEM((LEVELS + 2, 2, 2, 4, 64, 256), BF16),
-            pltpu.VMEM((LEVELS + 1, 2, 2, 64, 256), BF16),
+            pltpu.VMEM((WIDE + 1, 2, 2, 64, 256), BF16),
+            pltpu.VMEM((WIDE, 2, 2, 64, 256), BF16),
+            pltpu.VMEM((WIDE + 3, 2, 2, 4, 64, 256), BF16),
+            pltpu.VMEM((WIDE + 1, 2, 2, 64, 256), BF16),
+            pltpu.VMEM((2, 2, 64, 256), BF16),
+            pltpu.VMEM((2, 2, 64, 256), BF16),
+            pltpu.VMEM((2, 2, 64, 256), BF16),
             pltpu.VMEM((2, 16, 16, 128), BF16),
             pltpu.VMEM((32, 16, 128), BF16),
             dma((4, 2)), dma, dma((4, 2)), dma,
             dma((3, 4)), dma((3, 4)), dma((3,)), dma((3,)),
-            dma, dma, dma((LEVELS + 1,)), dma((LEVELS + 1,)),
-            dma((LEVELS,)), dma((LEVELS,)), dma((LEVELS + 1, 3)), dma((LEVELS + 1, 3)),
-            dma, dma((2, 16)),
+            dma((2,)), dma((2,)), dma((WIDE + 1,)), dma((WIDE + 1,)),
+            dma((WIDE,)), dma((WIDE,)), dma((WIDE + 3, 2, 3)), dma((WIDE + 3, 2, 3)),
+            dma((5,)), dma((5,)), dma, dma((2, 16)),
         ],
         compiler_params=pltpu.CompilerParams(
-            collective_id=0, has_side_effects=True, vmem_limit_bytes=40 * 1024 * 1024
+            collective_id=0, has_side_effects=True, vmem_limit_bytes=60 * 1024 * 1024
         ),
         cost_estimate=pl.CostEstimate(
             flops=8 * 512 * 512 * 512 * 3, bytes_accessed=4 * 1024 * 1024, transcendentals=0

time: 138 us -> 123 us (0.89)
  Pallas kernels: 134 us -> 119 us
    pallas_call x1, Pallas kernels: 134 us -> 119 us  [per_device(): pl.pallas_call(kernel, out_shape=jax.ShapeDtypeStruct((32, 16, 128), BF16...]
where the time goes in v2:
time: 123 us; the launch traced here: 122 us
  Pallas kernels  119 us (97%)
  local copies, waits for them, and re-layouts  1.62 us (1%)
    pallas_call x1, Pallas kernels, per_device(): pl.pallas_call(kernel, out_shape=jax.ShapeDtypeStruct((32, 16, 128), BF16...  119 us

profile of v2, /device:TPU:1, one launch (start us, length us, event | category | flops | bytes accessed | tf_op | source)
XLA Modules:
  0.0 122.1 jit_solution(6016267721931555205)
XLA Ops:
  0.0 118.6 %propagate.1 = bf16[32,16,128]{2,1,0:T(8,128)(2,1)} custom-call(bf16[1,2,512,512]{3,2,1,0:T(8,128)(2,1)} %x_ref.1), custom_call_target="tpu_custom_call" | custom-call | flops 3221225472 | bytes 4194304 | tf_op jit(solution)/shard_map/propagate/pallas_call | solution.py:324
  118.6 1.1 fusion.31
  119.7 0.2 reshape.11
  119.9 0.2 reshape.12
  120.0 0.2 fusion.9
  120.3 0.2 convolution_subtract_fusion
  120.5 0.2 fusion.11
  120.8 0.2 convolution_add_fusion
  121.0 0.1 stack.9
  121.1 0.1 stack.10
  121.2 0.9 fusion

commit v3 on v2

--- a/solution.py
+++ b/solution.py
@@ -47,7 +47,7 @@
     x_ref, o_ref,
     left, right, pairs, pair_low, chain, acc, ends, sibling, shifted, gathered, period,
     late_shift, late_sib, late, tiles, landed,
-    left_sem, right_sem, left_out, right_out, pair_sem, pair_out, chain_sem, chain_out,
+    left_sem, right_sem, left_out, right_out, pair_sem, pair_out, first_sem, first_out, chain_sem, chain_out,
     ends_sem, ends_out, sib_sem, sib_out, shift_sem, shift_out, gather_sem, gather_out,
     late_sem, late_out, all_sem, all_out,
 ):
@@ -104,6 +104,10 @@
 
     arrived(right, right_sem)
 
+    def pass_pair(r, d):
+        block = pairs.at[y, :, pl.ds(pl.multiple_of(128 * r, 128), 128)]
+        send(block, block, pair_out.at[d - 1, r], pair_sem.at[d - 1, r], along_y(d))
+
     def pair_chunk(r, carry):
         rows = pl.ds(pl.multiple_of(128 * r, 128), 128)
         for q in range(2):
@@ -115,30 +119,67 @@
             high, low = halves(part)
             pairs[y, i, rows, :] = high
             pair_low[i, rows, :] = low
-        for d in (1, 3, 2):
-            block = pairs.at[y, :, rows]
-            send(block, block, pair_out.at[d - 1, r], pair_sem.at[d - 1, r], along_y(d))
+
+        @pl.when(y != 3)
+        def _():
+            pass_pair(r, 1 + 2 * lax.rem(r, 2))
+
+        @pl.when(y == 3)
+        def _():
+            p = lax.div(r, 2)
+            for n in range(2):
+                chip = 2 * lax.rem(r, 2) + n
+                part = pl.ds(pl.multiple_of(128 * r + 64 * n, 64), 64)
+
+                @pl.when(chip != 3)
+                def _():
+                    for low, src in enumerate((pairs.at[3, :, part], pair_low.at[:, part])):
+                        send(
+                            src, chain.at[0, h, low, :, p],
+                            first_out.at[chip, low, p], first_sem.at[low, p],
+                            (c, xh * 8 + chip * 2 + h),
+                        )
+
         return carry
 
     lax.fori_loop(0, 4, pair_chunk, 0)
 
+    for r in range(4):
+        d = 1 if r % 2 == 0 else 3
+
+        @pl.when(y != (0 if d == 1 else 2))
+        def _():
+            block = pairs.at[lax.rem(y + 4 - d, 4), :, pl.ds(128 * r, 128)]
+            arrived(block, pair_sem.at[d - 1, r])
+            send(block, block, pair_out.at[1, r], pair_sem.at[1, r], along_y(d))
+
+        @pl.when(y != 3)
+        def _():
+            pass_pair(r, 4 - d)
+
     def wait_pair(j):
-        @pl.when(y != j)
-        def _():
-            d = lax.rem(y - j + 4, 4)
-            for r in range(4):
-                arrived(pairs.at[j, :, pl.ds(128 * r, 128)], pair_sem.at[d - 1, r])
+        for d, chunks in ((1, (1, 3)), (2, (0, 1, 2, 3)), (3, (0, 2))):
+            @pl.when(lax.rem(y - j + 4, 4) == d)
+            def _():
+                for r in chunks:
+                    arrived(pairs.at[j, :, pl.ds(128 * r, 128)], pair_sem.at[d - 1, r])
 
     def exchange_chain(s):
         send(chain.at[s, h], chain.at[s, h], chain_out.at[s], chain_sem.at[s], sib)
 
-    wait_pair(3)
-    for i in range(2):
+    @pl.when(y == 3)
+    def _():
         for p in range(2):
-            rows = pl.ds(pl.multiple_of(256 * p + 64 * y, 64), 64)
-            chain[0, h, 0, i, p] = pairs[3, i, rows, :]
-            low = pair_low[i, rows, :]
-            chain[0, h, 1, i, p] = jnp.where(y == 3, low, jnp.zeros_like(low))
+            rows = pl.ds(256 * p + 192, 64)
+            chain[0, h, 0, :, p] = pairs[3, :, rows, :]
+            chain[0, h, 1, :, p] = pair_low[:, rows, :]
+
+    @pl.when(y != 3)
+    def _():
+        for low in range(2):
+            for p in range(2):
+                arrived(chain.at[0, h, low, :, p], first_sem.at[low, p])
+
     exchange_chain(0)
     for s in range(3):
         j = 2 - s
@@ -277,9 +318,24 @@
             for q in range(2):
                 arrived(left.at[q, :, pl.ds(128 * r, 128)], left_out.at[r, q])
 
-    for d in range(3):
-        for r in range(4):
-            arrived(pairs.at[y, :, pl.ds(128 * r, 128)], pair_out.at[d, r])
+    @pl.when(y != 3)
+    def _():
+        for d in (1, 3):
+            for r in range(4):
+                arrived(pairs.at[y, :, pl.ds(128 * r, 128)], pair_out.at[d - 1, r])
+
+    @pl.when(y == 3)
+    def _():
+        for chip in range(3):
+            for low in range(2):
+                for p in range(2):
+                    arrived(pair_low.at[:, pl.ds(0, 64)], first_out.at[chip, low, p])
+
+    for r in range(4):
+        @pl.when(y != (0 if r % 2 == 0 else 2))
+        def _():
+            arrived(pairs.at[y, :, pl.ds(128 * r, 128)], pair_out.at[1, r])
+
     for s in range(3):
         arrived(chain.at[s, h], chain_out.at[s])
     for order in range(2):
@@ -344,7 +400,7 @@
             pltpu.VMEM((2, 16, 16, 128), BF16),
             pltpu.VMEM((32, 16, 128), BF16),
             dma((4, 2)), dma, dma((4, 2)), dma,
-            dma((3, 4)), dma((3, 4)), dma((3,)), dma((3,)),
+            dma((3, 4)), dma((3, 4)), dma((2, 2)), dma((3, 2, 2)), dma((3,)), dma((3,)),
             dma((2,)), dma((2,)), dma((WIDE + 1,)), dma((WIDE + 1,)),
             dma((WIDE,)), dma((WIDE,)), dma((WIDE + 3, 2, 3)), dma((WIDE + 3, 2, 3)),
             dma((5,)), dma((5,)), dma, dma((2, 16)),

time: 123 us -> 116 us (0.943)
  Pallas kernels: 119 us -> 112 us
    pallas_call x1, Pallas kernels: 119 us -> 112 us  [per_device(): pl.pallas_call(kernel, out_shape=jax.ShapeDtypeStruct((32, 16, 128), BF16...]
where the time goes in v3:
time: 116 us
  Pallas kernels  112 us (97%)
  local copies, waits for them, and re-layouts  1.62 us (1%)
    pallas_call x1, Pallas kernels, per_device(): pl.pallas_call(kernel, out_shape=jax.ShapeDtypeStruct((32, 16, 128), BF16...  112 us

profile of v3, /device:TPU:1, one launch (start us, length us, event | category | flops | bytes accessed | tf_op | source)
XLA Modules:
  0.0 115.7 jit_solution(5738122833235705903)
XLA Ops:
  0.0 112.2 %propagate.1 = bf16[32,16,128]{2,1,0:T(8,128)(2,1)} custom-call(bf16[1,2,512,512]{3,2,1,0:T(8,128)(2,1)} %x_ref.1), custom_call_target="tpu_custom_call" | custom-call | flops 3221225472 | bytes 4194304 | tf_op jit(solution)/shard_map/propagate/pallas_call | solution.py:380
  112.2 1.1 fusion.31
  113.3 0.2 reshape.11
  113.5 0.2 reshape.12
  113.6 0.2 fusion.9
  113.9 0.2 convolution_subtract_fusion
  114.1 0.2 fusion.11
  114.4 0.2 convolution_add_fusion
  114.6 0.1 stack.9
  114.7 0.1 stack.10
  114.8 0.9 fusion

commit v4 on v3

--- a/solution.py
+++ b/solution.py
@@ -45,11 +45,12 @@
 
 def kernel(
     x_ref, o_ref,
-    left, right, pairs, pair_low, chain, acc, ends, sibling, shifted, gathered, period,
-    late_shift, late_sib, late, tiles, landed,
+    left, right, pairs, pair_low, chain, acc, end_left, end_right, end_sib,
+    sibling, shifted, gathered, period, beside, turn, turn_sib, cross,
+    late_shift, late_sib, late, final, tiles, landed,
     left_sem, right_sem, left_out, right_out, pair_sem, pair_out, first_sem, first_out, chain_sem, chain_out,
-    ends_sem, ends_out, sib_sem, sib_out, shift_sem, shift_out, gather_sem, gather_out,
-    late_sem, late_out, all_sem, all_out,
+    ends_sem, ends_out, end_sib_sem, end_sib_out, sib_sem, sib_out, shift_sem, shift_out, gather_sem, gather_out,
+    turn_sem, turn_out, late_sem, late_out, final_sem, final_out, all_sem, all_out,
 ):
     c = lax.axis_index("cuts")
     b = lax.axis_index("blk")
@@ -66,6 +67,9 @@
     def cut(k):
         return (lax.rem(c + k + 32, 32), b)
 
+    def cut_over(k):
+        return (lax.rem(c + k + 32, 32), opposite[1])
+
     @pl.when(h == 0)
     def _():
         pltpu.make_async_copy(x_ref.at[0, :, :, pl.ds(0, 256)], right, right_sem).start()
@@ -82,6 +86,7 @@
 
     barrier = pltpu.get_barrier_semaphore()
     greet = [sib, opposite] + [along_y(d) for d in (1, 2, 3)] + [cut(1 << s) for s in range(LEVELS)]
+    greet += [cut_over(1 << s) for s in range(WIDE + 1)]
     for device in greet:
         pl.semaphore_signal(barrier, inc=1, device_id=device, device_id_type=MESH)
     pl.semaphore_wait(barrier, len(greet))
@@ -181,6 +186,7 @@
                 arrived(chain.at[0, h, low, :, p], first_sem.at[low, p])
 
     exchange_chain(0)
+    ends = []
     for s in range(3):
         j = 2 - s
         wait_pair(j)
@@ -201,80 +207,146 @@
             if s < 2:
                 chain[s + 1, h, 0, i], chain[s + 1, h, 1, i] = halves(part)
             else:
-                ends[xh, i] = part.astype(BF16)
+                ends.append(part.astype(BF16))
         if s < 2:
             exchange_chain(s + 1)
 
-    def spread(src, level, order, p):
+    @pl.when(xh == 0)
+    def _():
+        for q in range(2):
+            end_right[q] = jnp.concatenate([part[:, :, 128 * q : 128 * q + 128] for part in ends], axis=2)
+
+    @pl.when(xh == 1)
+    def _():
+        for i in range(2):
+            end_left[i] = ends[i]
+
+    def spread(src, level):
         for d in (1, 3, 2):
             send(
-                src, gathered.at[level, :, p, y],
-                gather_out.at[level, order, d - 1], gather_sem.at[level, order, d - 1], along_y(d),
+                src, gathered.at[level, :, y],
+                gather_out.at[level, d - 1], gather_sem.at[level, d - 1], along_y(d),
             )
 
-    def spread_arrived(level, order, p):
+    def spread_arrived(level):
         for d in (1, 2, 3):
-            arrived(gathered.at[level, :, p, lax.rem(y - d + 4, 4)], gather_sem.at[level, order, d - 1])
-
-    def half_product(x, level, p):
-        return [dot(x, gathered[level, i, p].reshape(256, 256)) for i in range(2)]
-
-    def product(own, theirs, theirs_sem, level):
-        rows = 2 * math.prod(own.shape[1:-1])
-        spread_arrived(level, 0, h)
-        by = half_product(own[...].reshape(rows, 256), level, h)
-        arrived(theirs, theirs_sem)
-        spread_arrived(level, 1, other)
-        more = half_product(theirs[...].reshape(rows, 256), level, other)
-        return combine(by[0] + more[0], by[1] + more[1])
-
-    def keep(parts, level):
-        for i, part in enumerate(parts):
-            part = part.reshape(2, 64, 256).astype(BF16)
-            period[level, i] = part
-            gathered[level + 1, i, :, y] = part
-
-    for order, p in enumerate((h, other)):
-        send(ends.at[xh, :, p], ends.at[xh, :, p], ends_out.at[order], ends_sem.at[order], opposite)
-    for order, p in enumerate((h, other)):
-        arrived(ends.at[1 - xh, :, p], ends_sem.at[order])
-        spread(ends.at[0, :, p], 0, order, p)
-    send(ends.at[1], sibling.at[0], sib_out.at[0], sib_sem.at[0], sib)
-    gathered[0, :, :, y] = ends[0]
-    keep(product(ends.at[1], sibling.at[0], sib_sem.at[0], 0), 0)
+            arrived(gathered.at[level, :, lax.rem(y - d + 4, 4)], gather_sem.at[level, d - 1])
+
+    def quarter_product(x, level, p):
+        return dot(x, gathered[level, p].reshape(256, 256))
+
+    def quarter(t):
+        rows = t.shape[0] // 2
+        return t[:rows, :128] - t[rows:, 128:], t[:rows, 128:] + t[rows:, :128]
+
+    def joined(blocks):
+        rows = math.prod(blocks.shape[1:-1])
+        return jnp.concatenate([blocks[0].reshape(rows, 128), blocks[1].reshape(rows, 128)], axis=1)
+
+    def keep(t, level):
+        parts = [part.reshape(2, 64, 128).astype(BF16) for part in quarter(t)]
+        for i in range(2):
+            period[level, i] = parts[i]
+        side = jnp.concatenate(parts, axis=2)
+        beside[level] = side
+        gathered[level + 1, :, y] = side
+
+    @pl.when(xh == 0)
+    def _():
+        send(end_right.at[1], end_right.at[0], ends_out, ends_sem, opposite)
+
+    @pl.when(xh == 1)
+    def _():
+        send(end_left, end_left, ends_out, ends_sem, opposite)
+        arrived(end_right.at[0], ends_sem)
+
+    spread(end_right.at[0], 0)
+    gathered[0, :, y] = end_right[0]
+
+    @pl.when(xh == 0)
+    def _():
+        arrived(end_left, ends_sem)
+
+    send(end_left, end_sib, end_sib_out, end_sib_sem, sib)
+    spread_arrived(0)
+    t = quarter_product(end_left[...].reshape(256, 256), 0, h)
+    arrived(end_sib, end_sib_sem)
+    keep(t + quarter_product(end_sib[...].reshape(256, 256), 0, other), 0)
 
     def double(level, k):
-        send(period.at[level], shifted.at[level], shift_out.at[level], shift_sem.at[level], cut(-k))
-        for order, p in enumerate((h, other)):
-            spread(period.at[level, :, p], level + 1, order, p)
-        arrived(shifted.at[level], shift_sem.at[level])
-        after = level + 1
-        send(shifted.at[level], sibling.at[after], sib_out.at[after], sib_sem.at[after], sib)
-        keep(product(shifted.at[level], sibling.at[after], sib_sem.at[after], after), after)
+        for n, device in enumerate((cut(-k), cut_over(-k))):
+            send(
+                period.at[level], shifted.at[level, xh],
+                shift_out.at[level, n], shift_sem.at[level, xh], device,
+            )
+        spread(beside.at[level], level + 1)
+        for q in (xh, 1 - xh):
+            arrived(shifted.at[level, q], shift_sem.at[level, q])
+            send(
+                shifted.at[level, q], sibling.at[level, q],
+                sib_out.at[level, q], sib_sem.at[level, q], sib,
+            )
+        spread_arrived(level + 1)
+        t = quarter_product(joined(shifted.at[level]), level + 1, h)
+        for q in range(2):
+            arrived(sibling.at[level, q], sib_sem.at[level, q])
+        keep(t + quarter_product(joined(sibling.at[level]), level + 1, other), level + 1)
         return 2 * k
 
     lax.fori_loop(0, WIDE, double, jnp.int32(1))
 
-    send(period.at[WIDE, :, xh], late_shift.at[0], late_out.at[0], late_sem.at[0], cut(-8))
-    for order, p in enumerate((h, other)):
-        spread(period.at[WIDE, :, p], WIDE + 1, order, p)
-    arrived(late_shift.at[0], late_sem.at[0])
-    send(late_shift.at[0], late_sib.at[0], late_out.at[1], late_sem.at[1], sib)
-    for i, part in enumerate(product(late_shift.at[0], late_sib.at[0], late_sem.at[1], WIDE + 1)):
-        part = part.astype(BF16)
+    for half in range(2):
+        send(
+            period.at[WIDE, :, half], turn.at[xh], turn_out.at[half], turn_sem.at[xh],
+            (lax.rem(c + 24, 32), half * 8 + y * 2 + h),
+        )
+    send(beside.at[WIDE], cross, late_out.at[0], late_sem.at[0], opposite)
+    spread(beside.at[WIDE], WIDE + 1)
+    arrived(cross, late_sem.at[0])
+    spread(cross, WIDE + 2)
+    gathered[WIDE + 2, :, y] = cross[...]
+    for q in range(2):
+        arrived(turn.at[q], turn_sem.at[q])
+    send(turn, turn_sib, late_out.at[1], late_sem.at[1], sib)
+    x0 = joined(turn)
+    spread_arrived(WIDE + 1)
+    own = quarter_product(x0, WIDE + 1, h)
+    arrived(turn_sib, late_sem.at[1])
+    x1 = joined(turn_sib)
+    own = quarter(own + quarter_product(x1, WIDE + 1, other))
+    spread_arrived(WIDE + 2)
+    far = quarter(quarter_product(x0, WIDE + 2, h) + quarter_product(x1, WIDE + 2, other))
+    for i in range(2):
+        first = jnp.where(xh == 0, own[i], far[i])
+        second = jnp.where(xh == 0, far[i], own[i])
+        part = jnp.concatenate([first, second], axis=1).astype(BF16)
         late[0, i] = part
-        gathered[WIDE + 2, i, xh, y] = part
-
-    send(late.at[0], late_shift.at[1], late_out.at[2], late_sem.at[2], cut(-16))
+        final[i, xh, y] = part
+
+    def spread_final(src, p, order):
+        for d in (1, 3, 2):
+            send(
+                src, final.at[:, p, y],
+                final_out.at[order, d - 1], final_sem.at[order, d - 1], along_y(d),
+            )
+
+    send(late.at[0], late_shift, late_out.at[2], late_sem.at[2], cut(-16))
     send(late.at[0], late.at[1], late_out.at[3], late_sem.at[3], opposite)
-    level = WIDE + 2
-    spread(late.at[0], level, lax.rem(xh + h, 2), xh)
+    spread_final(late.at[0], xh, 0)
     arrived(late.at[1], late_sem.at[3])
-    spread(late.at[1], level, lax.rem(1 - xh + h, 2), 1 - xh)
-    gathered[level, :, 1 - xh, y] = late[1]
-    arrived(late_shift.at[1], late_sem.at[2])
-    send(late_shift.at[1], late_sib.at[1], late_out.at[4], late_sem.at[4], sib)
-    real, imag = product(late_shift.at[1], late_sib.at[1], late_sem.at[4], level)
+    spread_final(late.at[1], 1 - xh, 1)
+    final[:, 1 - xh, y] = late[1]
+    arrived(late_shift, late_sem.at[2])
+    send(late_shift, late_sib, late_out.at[4], late_sem.at[4], sib)
+    for order, p in enumerate((xh, 1 - xh)):
+        for d in (1, 2, 3):
+            arrived(final.at[:, p, lax.rem(y - d + 4, 4)], final_sem.at[order, d - 1])
+    x0 = late_shift[...].reshape(128, 256)
+    by = [dot(x0, final[i, h].reshape(256, 256)) for i in range(2)]
+    arrived(late_sib, late_sem.at[4])
+    x1 = late_sib[...].reshape(128, 256)
+    by = [by[i] + dot(x1, final[i, other].reshape(256, 256)) for i in range(2)]
+    real, imag = combine(*by)
 
     stacked = jnp.concatenate([real[:32], imag[:32], real[32:], imag[32:]], axis=0)
     turned = stacked.T
@@ -338,30 +410,37 @@
 
     for s in range(3):
         arrived(chain.at[s, h], chain_out.at[s])
+    @pl.when(xh == 0)
+    def _():
+        arrived(end_right.at[1], ends_out)
+
+    @pl.when(xh == 1)
+    def _():
+        arrived(end_left, ends_out)
+
+    arrived(end_sib, end_sib_out)
+
+    def level_sent(level, carry):
+        for d in range(3):
+            arrived(gathered.at[level, :, y], gather_out.at[level, d])
+        return carry
+
+    lax.fori_loop(0, WIDE + 3, level_sent, 0)
+
+    def shift_sent(level, carry):
+        for n in range(2):
+            arrived(period.at[level], shift_out.at[level, n])
+            arrived(sibling.at[level, n], sib_out.at[level, n])
+        return carry
+
+    lax.fori_loop(0, WIDE, shift_sent, 0)
+    for half in range(2):
+        arrived(turn.at[half], turn_out.at[half])
+    for n in range(5):
+        arrived(cross if n == 0 else late.at[0], late_out.at[n])
     for order in range(2):
-        arrived(ends.at[xh, :, 0], ends_out.at[order])
-
-    def level_sent(level, carry):
-        for order in range(2):
-            for d in range(3):
-                arrived(gathered.at[level, :, 0, y], gather_out.at[level, order, d])
-        return carry
-
-    lax.fori_loop(0, WIDE + 3, level_sent, 0)
-
-    def shift_sent(level, carry):
-        arrived(period.at[level], shift_out.at[level])
-        return carry
-
-    lax.fori_loop(0, WIDE, shift_sent, 0)
-
-    def sibling_sent(level, carry):
-        arrived(sibling.at[level], sib_out.at[level])
-        return carry
-
-    lax.fori_loop(0, WIDE + 1, sibling_sent, 0)
-    for n in range(5):
-        arrived(late.at[0], late_out.at[n])
+        for d in range(3):
+            arrived(late.at[0], final_out.at[order, d])
 
     def scatter_sent(j, carry):
         for core in range(2):
@@ -389,21 +468,29 @@
             pltpu.VMEM((2, 512, 256), BF16),
             pltpu.VMEM((3, 2, 2, 2, 2, 64, 256), BF16),
             pltpu.VMEM((2, 256, 256), F32),
-            pltpu.VMEM((2, 2, 2, 64, 256), BF16),
-            pltpu.VMEM((WIDE + 1, 2, 2, 64, 256), BF16),
-            pltpu.VMEM((WIDE, 2, 2, 64, 256), BF16),
-            pltpu.VMEM((WIDE + 3, 2, 2, 4, 64, 256), BF16),
-            pltpu.VMEM((WIDE + 1, 2, 2, 64, 256), BF16),
             pltpu.VMEM((2, 2, 64, 256), BF16),
             pltpu.VMEM((2, 2, 64, 256), BF16),
             pltpu.VMEM((2, 2, 64, 256), BF16),
+            pltpu.VMEM((WIDE, 2, 2, 2, 64, 128), BF16),
+            pltpu.VMEM((WIDE, 2, 2, 2, 64, 128), BF16),
+            pltpu.VMEM((WIDE + 3, 2, 4, 64, 256), BF16),
+            pltpu.VMEM((WIDE + 1, 2, 2, 64, 128), BF16),
+            pltpu.VMEM((WIDE + 1, 2, 64, 256), BF16),
+            pltpu.VMEM((2, 2, 64, 128), BF16),
+            pltpu.VMEM((2, 2, 64, 128), BF16),
+            pltpu.VMEM((2, 64, 256), BF16),
+            pltpu.VMEM((2, 64, 256), BF16),
+            pltpu.VMEM((2, 64, 256), BF16),
+            pltpu.VMEM((2, 2, 64, 256), BF16),
+            pltpu.VMEM((2, 2, 4, 64, 256), BF16),
             pltpu.VMEM((2, 16, 16, 128), BF16),
             pltpu.VMEM((32, 16, 128), BF16),
             dma((4, 2)), dma, dma((4, 2)), dma,
             dma((3, 4)), dma((3, 4)), dma((2, 2)), dma((3, 2, 2)), dma((3,)), dma((3,)),
-            dma((2,)), dma((2,)), dma((WIDE + 1,)), dma((WIDE + 1,)),
-            dma((WIDE,)), dma((WIDE,)), dma((WIDE + 3, 2, 3)), dma((WIDE + 3, 2, 3)),
-            dma((5,)), dma((5,)), dma, dma((2, 16)),
+            dma, dma, dma, dma, dma((WIDE, 2)), dma((WIDE, 2)),
+            dma((WIDE, 2)), dma((WIDE, 2)), dma((WIDE + 3, 3)), dma((WIDE + 3, 3)),
+            dma((2,)), dma((2,)), dma((5,)), dma((5,)), dma((2, 3)), dma((2, 3)),
+            dma, dma((2, 16)),
         ],
         compiler_params=pltpu.CompilerParams(
             collective_id=0, has_side_effects=True, vmem_limit_bytes=60 * 1024 * 1024

time: 116 us -> 112 us (0.966)
  Pallas kernels: 112 us -> 108 us
    pallas_call x1, Pallas kernels: 112 us -> 108 us  [per_device(): pl.pallas_call(kernel, out_shape=jax.ShapeDtypeStruct((32, 16, 128), BF16...]
where the time goes in v4:
time: 112 us
  Pallas kernels  108 us (96%)
  local copies, waits for them, and re-layouts  1.62 us (1%)
    pallas_call x1, Pallas kernels, per_device(): pl.pallas_call(kernel, out_shape=jax.ShapeDtypeStruct((32, 16, 128), BF16...  108 us

profile of v4, /device:TPU:1, one launch (start us, length us, event | category | flops | bytes accessed | tf_op | source)
XLA Modules:
  0.0 111.6 jit_solution(8080318157581426484)
XLA Ops:
  0.0 108.1 %propagate.1 = bf16[32,16,128]{2,1,0:T(8,128)(2,1)} custom-call(bf16[1,2,512,512]{3,2,1,0:T(8,128)(2,1)} %x_ref.1), custom_call_target="tpu_custom_call" | custom-call | flops 3221225472 | bytes 4194304 | tf_op jit(solution)/shard_map/propagate/pallas_call | solution.py:459
  108.2 1.1 fusion.31
  109.2 0.2 reshape.11
  109.4 0.2 reshape.12
  109.6 0.2 fusion.9
  109.8 0.2 convolution_subtract_fusion
  110.0 0.2 fusion.11
  110.3 0.2 convolution_add_fusion
  110.5 0.1 stack.9
  110.6 0.1 stack.10
  110.7 0.9 fusion

commit v5 on v4

--- a/solution.py
+++ b/solution.py
@@ -50,7 +50,7 @@
     late_shift, late_sib, late, final, tiles, landed,
     left_sem, right_sem, left_out, right_out, pair_sem, pair_out, first_sem, first_out, chain_sem, chain_out,
     ends_sem, ends_out, end_sib_sem, end_sib_out, sib_sem, sib_out, shift_sem, shift_out, gather_sem, gather_out,
-    turn_sem, turn_out, late_sem, late_out, final_sem, final_out, all_sem, all_out,
+    turn_sem, turn_out, late_sem, late_out, final_sem, final_out, relay_sem, all_sem, all_out,
 ):
     c = lax.axis_index("cuts")
     b = lax.axis_index("blk")
@@ -85,11 +85,17 @@
                 ).start()
 
     barrier = pltpu.get_barrier_semaphore()
-    greet = [sib, opposite] + [along_y(d) for d in (1, 2, 3)] + [cut(1 << s) for s in range(LEVELS)]
-    greet += [cut_over(1 << s) for s in range(WIDE + 1)]
+    greet = [sib, opposite] + [along_y(d) for d in (1, 2, 3)]
+    greet += [cut(1), cut_over(1), cut(2), cut_over(2), cut(-2)]
     for device in greet:
         pl.semaphore_signal(barrier, inc=1, device_id=device, device_id_type=MESH)
     pl.semaphore_wait(barrier, len(greet))
+
+    def relay(n):
+        for way in (-1, 1):
+            pl.semaphore_signal(relay_sem.at[n], inc=1, device_id=cut(way * (2 << n)), device_id_type=MESH)
+
+    relay(0)
 
     @pl.when(h == 0)
     def _():
@@ -149,6 +155,9 @@
 
     lax.fori_loop(0, 4, pair_chunk, 0)
 
+    pl.semaphore_wait(relay_sem.at[0], 2)
+    relay(1)
+
     for r in range(4):
         d = 1 if r % 2 == 0 else 3
 
@@ -171,6 +180,9 @@
 
     def exchange_chain(s):
         send(chain.at[s, h], chain.at[s, h], chain_out.at[s], chain_sem.at[s], sib)
+
+    pl.semaphore_wait(relay_sem.at[1], 2)
+    relay(2)
 
     @pl.when(y == 3)
     def _():
@@ -250,6 +262,8 @@
         side = jnp.concatenate(parts, axis=2)
         beside[level] = side
         gathered[level + 1, :, y] = side
+
+    pl.semaphore_wait(relay_sem.at[2], 2)
 
     @pl.when(xh == 0)
     def _():
@@ -348,11 +362,10 @@
     by = [by[i] + dot(x1, final[i, other].reshape(256, 256)) for i in range(2)]
     real, imag = combine(*by)
 
-    stacked = jnp.concatenate([real[:32], imag[:32], real[32:], imag[32:]], axis=0)
-    turned = stacked.T
-    tiles[0] = turned.astype(BF16).reshape(16, 16, 128)
-    turned = jnp.concatenate([turned[:, 64:], turned[:, :64]], axis=1)
-    tiles[1] = turned.astype(BF16).reshape(16, 16, 128)
+    for core in range(2):
+        re, im = (v[32 * core : 32 * core + 32] for v in (real, imag))
+        turned = jnp.concatenate([re, im, im, -re], axis=0).T
+        tiles[core] = turned.astype(BF16).reshape(16, 16, 128)
     same = lax.div(c, 16) == h
 
     def nearness(t):
@@ -452,6 +465,30 @@
     lax.fori_loop(0, 16, scatter_sent, 0)
     arrived(landed, all_sem)
     o_ref[...] = landed[...]
+
+
+def sidebands(x_ref, o_ref):
+    lane = lax.broadcasted_iota(jnp.int32, (16, 128), 1)
+    sign = jnp.where(lane < 64, 1.0, -1.0).astype(F32)
+    terms = [x_ref[int(format(n, "05b")[::-1], 2)].astype(F32) for n in range(32)]
+    span = 1
+    while span < 32:
+        for start in range(0, 32, 2 * span):
+            for n in range(start, start + span):
+                angle = math.pi * (n - start) / span
+                upper = terms[n + span]
+                if n > start:
+                    quarter_turn = pltpu.roll(upper, 64, 1) * sign
+                    if 2 * (n - start) == span:
+                        upper = quarter_turn
+                    else:
+                        upper = math.cos(angle) * upper + math.sin(angle) * quarter_turn
+                terms[n], terms[n + span] = terms[n] + upper, terms[n] - upper
+        span *= 2
+    for n, term in enumerate(terms):
+        term = term * math.sqrt(512 / 32)
+        o_ref[n, 0] = term[:, :32]
+        o_ref[n, 1] = term[:, 32:64]
 
 
 def per_device(steps):
@@ -490,7 +527,7 @@
             dma, dma, dma, dma, dma((WIDE, 2)), dma((WIDE, 2)),
             dma((WIDE, 2)), dma((WIDE, 2)), dma((WIDE + 3, 3)), dma((WIDE + 3, 3)),
             dma((2,)), dma((2,)), dma((5,)), dma((5,)), dma((2, 3)), dma((2, 3)),
-            dma, dma((2, 16)),
+            pltpu.SemaphoreType.REGULAR((3,)), dma, dma((2, 16)),
         ],
         compiler_params=pltpu.CompilerParams(
             collective_id=0, has_side_effects=True, vmem_limit_bytes=60 * 1024 * 1024
@@ -500,18 +537,15 @@
         ),
         name="propagate",
     )(steps)
-    count = 32
-    index = jnp.arange(count, dtype=jnp.int32)
-    angle = 2.0 * math.pi / count * (index[:, None] * index[None, :] % count).astype(F32)
-    cosine, sine = jnp.cos(angle), jnp.sin(angle)
-    values = landed.astype(F32)
-    real_in = values[:, :, :32].reshape(count, 512)
-    imag_in = values[:, :, 32:64].reshape(count, 512)
-    hp = lax.Precision.HIGHEST
-    real = jnp.dot(cosine, real_in, precision=hp) + jnp.dot(sine, imag_in, precision=hp)
-    imag = jnp.dot(cosine, imag_in, precision=hp) - jnp.dot(sine, real_in, precision=hp)
-    result = jnp.stack([real, imag], axis=1) * math.sqrt(512 / count)
-    return result.reshape(count, 2, 16, 32).transpose(0, 1, 3, 2)
+    result = pl.pallas_call(
+        sidebands,
+        out_shape=jax.ShapeDtypeStruct((32, 2, 16, 32), F32),
+        in_specs=[pl.BlockSpec(memory_space=pltpu.VMEM)],
+        out_specs=pl.BlockSpec(memory_space=pltpu.VMEM),
+        compiler_params=pltpu.CompilerParams(vmem_limit_bytes=16 * 1024 * 1024),
+        name="sidebands",
+    )(landed)
+    return result.transpose(0, 1, 3, 2)
 
 
 def solution(mesh):

time: 112 us -> 108 us (0.964)
    pallas_call x1, Pallas kernels: 108 us -> 106 us  [per_device(): pl.pallas_call(kernel, out_shape=jax.ShapeDtypeStruct((32, 16, 128), BF16...]
    pallas_call x0 -> x1, Pallas kernels: none -> 1.2 us  [per_device(): pl.pallas_call(sidebands, out_shape=jax.ShapeDtypeStruct((32, 2, 16, 32),...]
where the time goes in v5:
time: 108 us
  Pallas kernels  107 us (99%)
    pallas_call x1, Pallas kernels, per_device(): pl.pallas_call(kernel, out_shape=jax.ShapeDtypeStruct((32, 16, 128), BF16...  106 us

profile of v5, /device:TPU:1, one launch (start us, length us, event | category | flops | bytes accessed | tf_op | source)
XLA Modules:
  0.0 108.0 jit_solution(6547623356849436081)
XLA Ops:
  0.0 105.9 %propagate.1.x_ref = bf16[32,16,128]{2,1,0:T(8,128)(2,1)} custom-call(bf16[1,2,512,512]{3,2,1,0:T(8,128)(2,1)} %x_ref.1), custom_call_target="tpu_custom_call" | custom-call | flops 3221225472 | bytes 4194304 | tf_op jit(solution)/shard_map/propagate/pallas_call | solution.py:496
  105.9 0.0 copy-start
  105.9 0.9 copy-done
  106.8 1.2 %sidebands.1 = f32[32,2,16,32]{3,2,1,0:T(8,128)} custom-call(bf16[32,16,128]{2,1,0:T(8,128)(2,1)S(1)} %copy-done), custom_call_target="tpu_custom_call" | custom-call | tf_op jit(solution)/shard_map/sidebands/pallas_call | solution.py:540
Async XLA Ops:
  105.9 0.9 copy-start

commit v6 on v5

v6 whole, which is shorter than its diff:
```python
import math

import jax
import jax.numpy as jnp
from jax import lax
from jax.experimental import pallas as pl
from jax.experimental.pallas import tpu as pltpu
from jax.sharding import PartitionSpec as P

MESH = pl.DeviceIdType.MESH
F32 = jnp.float32
BF16 = jnp.bfloat16
LEVELS = 5
WIDE = 3


def dot(a, b):
    return jnp.dot(a, b, preferred_element_type=F32)


def arrived(ref, sem):
    pltpu.make_async_copy(ref, ref, sem).wait()


def send(src, dst, send_sem, recv_sem, device):
    pltpu.make_async_remote_copy(
        src_ref=src,
        dst_ref=dst,
        send_sem=send_sem,
        recv_sem=recv_sem,
        device_id=device,
        device_id_type=MESH,
    ).start()


def combine(by_real, by_imag):
    rows = by_real.shape[0] // 2
    return by_real[:rows] - by_imag[rows:], by_imag[:rows] + by_real[rows:]


def halves(value):
    high = value.astype(BF16)
    return high, (value - high.astype(F32)).astype(BF16)


def sidebands(x_ref, o_ref):
    lane = lax.broadcasted_iota(jnp.int32, (16, 128), 1)
    sign = jnp.where(lane < 64, 1.0, -1.0).astype(F32)
    terms = [x_ref[int(format(n, "05b")[::-1], 2)].astype(F32) for n in range(32)]
    span = 1
    while span < 32:
        for start in range(0, 32, 2 * span):
            for n in range(start, start + span):
                angle = math.pi * (n - start) / span
                upper = terms[n + span]
                if n > start:
                    quarter_turn = pltpu.roll(upper, 64, 1) * sign
                    if 2 * (n - start) == span:
                        upper = quarter_turn
                    else:
                        upper = math.cos(angle) * upper + math.sin(angle) * quarter_turn
                terms[n], terms[n + span] = terms[n] + upper, terms[n] - upper
        span *= 2
    for n, term in enumerate(terms):
        term = term * math.sqrt(512 / 32)
        o_ref[n, 0] = term[:, :32]
        o_ref[n, 1] = term[:, 32:64]


def kernel(
    x_ref, o_ref,
    left, right, pairs, pair_low, chain, acc, end_left, end_right, end_sib,
    sibling, shifted, gathered, period, beside, turn, turn_sib, cross,
    late_shift, late_sib, late, final, tiles, landed,
    left_sem, right_sem, left_out, right_out, pair_sem, pair_out, first_sem, first_out, chain_sem, chain_out,
    ends_sem, ends_out, end_sib_sem, end_sib_out, sib_sem, sib_out, shift_sem, shift_out, gather_sem, gather_out,
    turn_sem, turn_out, late_sem, late_out, final_sem, final_out, relay_sem, all_sem, all_out,
):
    c = lax.axis_index("cuts")
    b = lax.axis_index("blk")
    xh = lax.div(b, 8)
    y = lax.rem(lax.div(b, 2), 4)
    h = lax.rem(b, 2)
    other = 1 - h
    sib = (c, b + 1 - 2 * h)
    opposite = (c, b + 8 - 16 * xh)

    def along_y(d):
        return (c, xh * 8 + lax.rem(y + d, 4) * 2 + h)

    def cut(k):
        return (lax.rem(c + k + 32, 32), b)

    def cut_over(k):
        return (lax.rem(c + k + 32, 32), opposite[1])

    @pl.when(h == 0)
    def _():
        pltpu.make_async_copy(x_ref.at[0, :, :, pl.ds(0, 256)], right, right_sem).start()

    @pl.when(h == 1)
    def _():
        for r in range(4):
            for q in range(2):
                pltpu.make_async_copy(
                    x_ref.at[0, :, pl.ds(128 * r, 128), pl.ds(256 * q, 256)],
                    left.at[q, :, pl.ds(128 * r, 128)],
                    left_sem.at[r, q],
                ).start()

    barrier = pltpu.get_barrier_semaphore()
    greet = [sib, opposite] + [along_y(d) for d in (1, 2, 3)]
    greet += [cut(1), cut_over(1), cut(2), cut_over(2), cut(-2)]
    for device in greet:
        pl.semaphore_signal(barrier, inc=1, device_id=device, device_id_type=MESH)
    pl.semaphore_wait(barrier, len(greet))

    def relay(n):
        for way in (-1, 1):
            pl.semaphore_signal(relay_sem.at[n], inc=1, device_id=cut(way * (2 << n)), device_id_type=MESH)

    relay(0)

    @pl.when(h == 0)
    def _():
        send(x_ref.at[0, :, :, pl.ds(256, 256)], right, right_out, right_sem, sib)

    @pl.when(h == 1)
    def _():
        for r in range(4):
            for q in range(2):
                send(
                    x_ref.at[0, :, pl.ds(128 * r, 128), pl.ds(256 * q, 256)],
                    left.at[q, :, pl.ds(128 * r, 128)],
                    left_out.at[r, q],
                    left_sem.at[r, q],
                    sib,
                )

    arrived(right, right_sem)

    def pass_pair(r, d):
        block = pairs.at[y, :, pl.ds(pl.multiple_of(128 * r, 128), 128)]
        send(block, block, pair_out.at[d - 1, r], pair_sem.at[d - 1, r], along_y(d))

    def pair_chunk(r, carry):
        rows = pl.ds(pl.multiple_of(128 * r, 128), 128)
        for q in range(2):
            arrived(left.at[q, :, rows], left_sem.at[r, q])
        x0 = left[0, :, rows, :].reshape(256, 256)
        x1 = left[1, :, rows, :].reshape(256, 256)
        by = [dot(x0, right[i, :256]) + dot(x1, right[i, 256:]) for i in range(2)]
        for i, part in enumerate(combine(*by)):
            high, low = halves(part)
            pairs[y, i, rows, :] = high
            pair_low[i, rows, :] = low

        @pl.when(y != 3)
        def _():
            pass_pair(r, 1 + 2 * lax.rem(r, 2))

        @pl.when(y == 3)
        def _():
            p = lax.div(r, 2)
            for n in range(2):
                chip = 2 * lax.rem(r, 2) + n
                part = pl.ds(pl.multiple_of(128 * r + 64 * n, 64), 64)

                @pl.when(chip != 3)
                def _():
                    for low, src in enumerate((pairs.at[3, :, part], pair_low.at[:, part])):
                        send(
                            src, chain.at[0, h, low, :, p],
                            first_out.at[chip, low, p], first_sem.at[low, p],
                            (c, xh * 8 + chip * 2 + h),
                        )

        return carry

    lax.fori_loop(0, 4, pair_chunk, 0)

    pl.semaphore_wait(relay_sem.at[0], 2)
    relay(1)

    for r in range(4):
        d = 1 if r % 2 == 0 else 3

        @pl.when(y != (0 if d == 1 else 2))
        def _():
            block = pairs.at[lax.rem(y + 4 - d, 4), :, pl.ds(128 * r, 128)]
            arrived(block, pair_sem.at[d - 1, r])
            send(block, block, pair_out.at[1, r], pair_sem.at[1, r], along_y(d))

        @pl.when(y != 3)
        def _():
            pass_pair(r, 4 - d)

    def wait_pair(j):
        for d, chunks in ((1, (1, 3)), (2, (0, 1, 2, 3)), (3, (0, 2))):
            @pl.when(lax.rem(y - j + 4, 4) == d)
            def _():
                for r in chunks:
                    arrived(pairs.at[j, :, pl.ds(128 * r, 128)], pair_sem.at[d - 1, r])

    def exchange_chain(s):
        send(chain.at[s, h], chain.at[s, h], chain_out.at[s], chain_sem.at[s], sib)

    pl.semaphore_wait(relay_sem.at[1], 2)
    relay(2)

    @pl.when(y == 3)
    def _():
        for p in range(2):
            rows = pl.ds(256 * p + 192, 64)
            chain[0, h, 0, :, p] = pairs[3, :, rows, :]
            chain[0, h, 1, :, p] = pair_low[:, rows, :]

    @pl.when(y != 3)
    def _():
        for low in range(2):
            for p in range(2):
                arrived(chain.at[0, h, low, :, p], first_sem.at[low, p])

    exchange_chain(0)
    ends = []
    for s in range(3):
        j = 2 - s
        wait_pair(j)
        for q in (h, other):
            if q is other:
                arrived(chain.at[s, other], chain_sem.at[s])
            rows = pl.ds(pl.multiple_of(256 * q, 256), 256)
            x = chain[s, q].reshape(512, 256)
            for i in range(2):
                t = dot(x, pairs[j, i, rows, :])
                t = t[:256] + t[256:]
                if q is h:
                    acc[i] = t
                else:
                    acc[i] += t

            @pl.when(y == j)
            def _():
                for i in range(2):
                    acc[i] += dot(x[:256], pair_low[i, rows, :])

        for i, part in enumerate(combine(acc[0], acc[1])):
            part = part.reshape(2, 64, 256)
            if s < 2:
                chain[s + 1, h, 0, i], chain[s + 1, h, 1, i] = halves(part)
            else:
                ends.append(part.astype(BF16))
        if s < 2:
            exchange_chain(s + 1)

    @pl.when(xh == 0)
    def _():
        for q in range(2):
            end_right[q] = jnp.concatenate([part[:, :, 128 * q : 128 * q + 128] for part in ends], axis=2)

    @pl.when(xh == 1)
    def _():
        for i in range(2):
            end_left[i] = ends[i]

    def spread(src, level):
        for d in (1, 3, 2):
            send(
                src, gathered.at[level, :, y],
                gather_out.at[level, d - 1], gather_sem.at[level, d - 1], along_y(d),
            )

    def spread_arrived(level):
        for d in (1, 2, 3):
            arrived(gathered.at[level, :, lax.rem(y - d + 4, 4)], gather_sem.at[level, d - 1])

    def quarter_product(x, level, p):
        return dot(x, gathered[level, p].reshape(256, 256))

    def quarter(t):
        rows = t.shape[0] // 2
        return t[:rows, :128] - t[rows:, 128:], t[:rows, 128:] + t[rows:, :128]

    def joined(blocks):
        rows = math.prod(blocks.shape[1:-1])
        return jnp.concatenate([blocks[0].reshape(rows, 128), blocks[1].reshape(rows, 128)], axis=1)

    def keep(t, level):
        parts = [part.reshape(2, 64, 128).astype(BF16) for part in quarter(t)]
        for i in range(2):
            period[level, i] = parts[i]
        side = jnp.concatenate(parts, axis=2)
        beside[level] = side
        gathered[level + 1, :, y] = side

    pl.semaphore_wait(relay_sem.at[2], 2)

    @pl.when(xh == 0)
    def _():
        send(end_right.at[1], end_right.at[0], ends_out, ends_sem, opposite)

    @pl.when(xh == 1)
    def _():
        send(end_left, end_left, ends_out, ends_sem, opposite)
        arrived(end_right.at[0], ends_sem)

    spread(end_right.at[0], 0)
    gathered[0, :, y] = end_right[0]

    @pl.when(xh == 0)
    def _():
        arrived(end_left, ends_sem)

    send(end_left, end_sib, end_sib_out, end_sib_sem, sib)
    spread_arrived(0)
    t = quarter_product(end_left[...].reshape(256, 256), 0, h)
    arrived(end_sib, end_sib_sem)
    keep(t + quarter_product(end_sib[...].reshape(256, 256), 0, other), 0)

    def double(level, k):
        for n, device in enumerate((cut_over(-k), cut(-k))):
            send(
                period.at[level], shifted.at[level, xh],
                shift_out.at[level, n], shift_sem.at[level, xh], device,
            )
        spread(beside.at[level], level + 1)
        for q in (xh, 1 - xh):
            arrived(shifted.at[level, q], shift_sem.at[level, q])
            send(
                shifted.at[level, q], sibling.at[level, q],
                sib_out.at[level, q], sib_sem.at[level, q], sib,
            )
        spread_arrived(level + 1)
        t = quarter_product(joined(shifted.at[level]), level + 1, h)
        for q in range(2):
            arrived(sibling.at[level, q], sib_sem.at[level, q])
        keep(t + quarter_product(joined(sibling.at[level]), level + 1, other), level + 1)
        return 2 * k

    lax.fori_loop(0, WIDE, double, jnp.int32(1))

    send(beside.at[WIDE], cross, late_out.at[0], late_sem.at[0], opposite)
    for half in (1 - xh, xh):
        send(
            period.at[WIDE, :, half], turn.at[xh], turn_out.at[half], turn_sem.at[xh],
            (lax.rem(c + 24, 32), half * 8 + y * 2 + h),
        )
    spread(beside.at[WIDE], WIDE + 1)
    arrived(cross, late_sem.at[0])
    spread(cross, WIDE + 2)
    gathered[WIDE + 2, :, y] = cross[...]
    for q in range(2):
        arrived(turn.at[q], turn_sem.at[q])
    send(turn, turn_sib, late_out.at[1], late_sem.at[1], sib)
    x0 = joined(turn)
    spread_arrived(WIDE + 1)
    own = quarter_product(x0, WIDE + 1, h)
    arrived(turn_sib, late_sem.at[1])
    x1 = joined(turn_sib)
    own = quarter(own + quarter_product(x1, WIDE + 1, other))
    spread_arrived(WIDE + 2)
    far = quarter(quarter_product(x0, WIDE + 2, h) + quarter_product(x1, WIDE + 2, other))
    for i in range(2):
        first = jnp.where(xh == 0, own[i], far[i])
        second = jnp.where(xh == 0, far[i], own[i])
        part = jnp.concatenate([first, second], axis=1).astype(BF16)
        late[0, i] = part
        final[i, xh, y] = part

    def spread_final(src, p, order):
        for d in (1, 3, 2):
            send(
                src, final.at[:, p, y],
                final_out.at[order, d - 1], final_sem.at[order, d - 1], along_y(d),
            )

    send(late.at[0], late_shift, late_out.at[2], late_sem.at[2], cut(-16))
    send(late.at[0], late.at[1], late_out.at[3], late_sem.at[3], opposite)
    spread_final(late.at[0], xh, 0)
    arrived(late.at[1], late_sem.at[3])
    spread_final(late.at[1], 1 - xh, 1)
    final[:, 1 - xh, y] = late[1]
    arrived(late_shift, late_sem.at[2])
    send(late_shift, late_sib, late_out.at[4], late_sem.at[4], sib)
    for order, p in enumerate((xh, 1 - xh)):
        for d in (1, 2, 3):
            arrived(final.at[:, p, lax.rem(y - d + 4, 4)], final_sem.at[order, d - 1])
    x0 = late_shift[...].reshape(128, 256)
    by = [dot(x0, final[i, h].reshape(256, 256)) for i in range(2)]
    arrived(late_sib, late_sem.at[4])
    x1 = late_sib[...].reshape(128, 256)
    by = [by[i] + dot(x1, final[i, other].reshape(256, 256)) for i in range(2)]
    real, imag = combine(*by)

    for core in range(2):
        re, im = (v[32 * core : 32 * core + 32] for v in (real, imag))
        turned = jnp.concatenate([re, im, im, -re], axis=0).T
        tiles[core] = turned.astype(BF16).reshape(16, 16, 128)
    same = lax.div(c, 16) == h

    def nearness(t):
        t = jnp.where(same, 15 - t, t)
        step = lax.div(t + 1, 2)
        return lax.rem(c + jnp.where(lax.rem(t, 2) == 1, step, 16 - step), 16)

    def scatter(t, carry):
        j = nearness(t)
        target = 16 * h + j
        for core in range(2):
            here = (target == c) & (h == core)

            @pl.when(here)
            def _():
                pltpu.make_async_copy(tiles.at[core, j], landed.at[c], all_sem).start()

            @pl.when(jnp.logical_not(here))
            def _():
                send(
                    tiles.at[core, j], landed.at[c], all_out.at[core, j], all_sem,
                    (target, xh * 8 + y * 2 + core),
                )
        return carry

    lax.fori_loop(0, 16, scatter, 0)

    @pl.when(h == 0)
    def _():
        arrived(right, right_out)

    @pl.when(h == 1)
    def _():
        for r in range(4):
            for q in range(2):
                arrived(left.at[q, :, pl.ds(128 * r, 128)], left_out.at[r, q])

    @pl.when(y != 3)
    def _():
        for d in (1, 3):
            for r in range(4):
                arrived(pairs.at[y, :, pl.ds(128 * r, 128)], pair_out.at[d - 1, r])

    @pl.when(y == 3)
    def _():
        for chip in range(3):
            for low in range(2):
                for p in range(2):
                    arrived(pair_low.at[:, pl.ds(0, 64)], first_out.at[chip, low, p])

    for r in range(4):
        @pl.when(y != (0 if r % 2 == 0 else 2))
        def _():
            arrived(pairs.at[y, :, pl.ds(128 * r, 128)], pair_out.at[1, r])

    for s in range(3):
        arrived(chain.at[s, h], chain_out.at[s])
    @pl.when(xh == 0)
    def _():
        arrived(end_right.at[1], ends_out)

    @pl.when(xh == 1)
    def _():
        arrived(end_left, ends_out)

    arrived(end_sib, end_sib_out)

    def level_sent(level, carry):
        for d in range(3):
            arrived(gathered.at[level, :, y], gather_out.at[level, d])
        return carry

    lax.fori_loop(0, WIDE + 3, level_sent, 0)

    def shift_sent(level, carry):
        for n in range(2):
            arrived(period.at[level], shift_out.at[level, n])
            arrived(sibling.at[level, n], sib_out.at[level, n])
        return carry

    lax.fori_loop(0, WIDE, shift_sent, 0)
    for half in range(2):
        arrived(turn.at[half], turn_out.at[half])
    for n in range(5):
        arrived(cross if n == 0 else late.at[0], late_out.at[n])
    for order in range(2):
        for d in range(3):
            arrived(late.at[0], final_out.at[order, d])

    def scatter_sent(j, carry):
        for core in range(2):
            @pl.when(jnp.logical_not((16 * h + j == c) & (h == core)))
            def _():
                arrived(tiles.at[core, j], all_out.at[core, j])
        return carry

    lax.fori_loop(0, 16, scatter_sent, 0)
    arrived(landed, all_sem)
    sidebands(landed, o_ref)


def per_device(steps):
    dma = pltpu.SemaphoreType.DMA
    result = pl.pallas_call(
        kernel,
        out_shape=jax.ShapeDtypeStruct((32, 2, 16, 32), F32),
        in_specs=[pl.BlockSpec(memory_space=pl.ANY)],
        out_specs=pl.BlockSpec(memory_space=pltpu.VMEM),
        scratch_shapes=[
            pltpu.VMEM((2, 2, 512, 256), BF16),
            pltpu.VMEM((2, 512, 256), BF16),
            pltpu.VMEM((4, 2, 512, 256), BF16),
            pltpu.VMEM((2, 512, 256), BF16),
            pltpu.VMEM((3, 2, 2, 2, 2, 64, 256), BF16),
            pltpu.VMEM((2, 256, 256), F32),
            pltpu.VMEM((2, 2, 64, 256), BF16),
            pltpu.VMEM((2, 2, 64, 256), BF16),
            pltpu.VMEM((2, 2, 64, 256), BF16),
            pltpu.VMEM((WIDE, 2, 2, 2, 64, 128), BF16),
            pltpu.VMEM((WIDE, 2, 2, 2, 64, 128), BF16),
            pltpu.VMEM((WIDE + 3, 2, 4, 64, 256), BF16),
            pltpu.VMEM((WIDE + 1, 2, 2, 64, 128), BF16),
            pltpu.VMEM((WIDE + 1, 2, 64, 256), BF16),
            pltpu.VMEM((2, 2, 64, 128), BF16),
            pltpu.VMEM((2, 2, 64, 128), BF16),
            pltpu.VMEM((2, 64, 256), BF16),
            pltpu.VMEM((2, 64, 256), BF16),
            pltpu.VMEM((2, 64, 256), BF16),
            pltpu.VMEM((2, 2, 64, 256), BF16),
            pltpu.VMEM((2, 2, 4, 64, 256), BF16),
            pltpu.VMEM((2, 16, 16, 128), BF16),
            pltpu.VMEM((32, 16, 128), BF16),
            dma((4, 2)), dma, dma((4, 2)), dma,
            dma((3, 4)), dma((3, 4)), dma((2, 2)), dma((3, 2, 2)), dma((3,)), dma((3,)),
            dma, dma, dma, dma, dma((WIDE, 2)), dma((WIDE, 2)),
            dma((WIDE, 2)), dma((WIDE, 2)), dma((WIDE + 3, 3)), dma((WIDE + 3, 3)),
            dma((2,)), dma((2,)), dma((5,)), dma((5,)), dma((2, 3)), dma((2, 3)),
            pltpu.SemaphoreType.REGULAR((3,)), dma, dma((2, 16)),
        ],
        compiler_params=pltpu.CompilerParams(
            collective_id=0, has_side_effects=True, vmem_limit_bytes=60 * 1024 * 1024
        ),
        cost_estimate=pl.CostEstimate(
            flops=8 * 512 * 512 * 512 * 3, bytes_accessed=4 * 1024 * 1024, transcendentals=0
        ),
        name="propagate",
    )(steps)
    return result.transpose(0, 1, 3, 2)


def solution(mesh):
    return jax.shard_map(
        per_device,
        mesh=mesh,
        in_specs=(P(("cuts", "blk"), None, None, None),),
        out_specs=P(None, None, "blk", "cuts"),
        check_vma=False,
    )
```

time: 108 us -> 106 us (0.981)
  Pallas kernels: 107 us -> 104 us
    pallas_call x2 -> x1, Pallas kernels: 107 us -> 104 us  [per_device(): pl.pallas_call(kernel, out_shape=jax.ShapeDtypeStruct((32, 2, 16, 32), F3...]
where the time goes in v6:
time: 106 us; the launch traced here: 105 us
  Pallas kernels  104 us (98%)
  local copies, waits for them, and re-layouts  1.87 us (2%)
    pallas_call x1, Pallas kernels, per_device(): pl.pallas_call(kernel, out_shape=jax.ShapeDtypeStruct((32, 2, 16, 32), F3...  104 us

profile of v6, /device:TPU:1, one launch (start us, length us, event | category | flops | bytes accessed | tf_op | source)
XLA Modules:
  0.0 105.5 jit_solution(16270449285500801904)
XLA Ops:
  0.0 103.6 %propagate.1 = f32[32,2,16,32]{3,2,1,0:T(8,128)} custom-call(bf16[1,2,512,512]{3,2,1,0:T(8,128)(2,1)} %x_ref.1), custom_call_target="tpu_custom_call" | custom-call | flops 3221225472 | bytes 4194304 | tf_op jit(solution)/shard_map/propagate/pallas_call | solution.py:502
  103.6 1.9 %copy.3 = f32[32,2,32,16]{2,3,1,0:T(8,128)} copy(f32[32,2,32,16]{2,3,1,0:T(8,128)} %bitcast.1) | data formatting | bytes 262144

commit v7 on v6

--- a/solution.py
+++ b/solution.py
@@ -203,7 +203,9 @@
                     arrived(pairs.at[j, :, pl.ds(128 * r, 128)], pair_sem.at[d - 1, r])
 
     def exchange_chain(s):
-        send(chain.at[s, h], chain.at[s, h], chain_out.at[s], chain_sem.at[s], sib)
+        for low in range(2):
+            part = chain.at[s, h, low]
+            send(part, part, chain_out.at[s, low], chain_sem.at[s, low], sib)
 
     pl.semaphore_wait(relay_sem.at[1], 2)
     relay(2)
@@ -228,7 +230,8 @@
         wait_pair(j)
         for q in (h, other):
             if q is other:
-                arrived(chain.at[s, other], chain_sem.at[s])
+                for low in range(2):
+                    arrived(chain.at[s, other, low], chain_sem.at[s, low])
             rows = pl.ds(pl.multiple_of(256 * q, 256), 256)
             x = chain[s, q].reshape(512, 256)
             for i in range(2):
@@ -452,7 +455,8 @@
             arrived(pairs.at[y, :, pl.ds(128 * r, 128)], pair_out.at[1, r])
 
     for s in range(3):
-        arrived(chain.at[s, h], chain_out.at[s])
+        for low in range(2):
+            arrived(chain.at[s, h, low], chain_out.at[s, low])
     @pl.when(xh == 0)
     def _():
         arrived(end_right.at[1], ends_out)
@@ -529,7 +533,7 @@
             pltpu.VMEM((2, 16, 16, 128), BF16),
             pltpu.VMEM((32, 16, 128), BF16),
             dma((4, 2)), dma, dma((4, 2)), dma,
-            dma((3, 4)), dma((3, 4)), dma((2, 2)), dma((3, 2, 2)), dma((3,)), dma((3,)),
+            dma((3, 4)), dma((3, 4)), dma((2, 2)), dma((3, 2, 2)), dma((3, 2)), dma((3, 2)),
             dma, dma, dma, dma, dma((WIDE, 2)), dma((WIDE, 2)),
             dma((WIDE, 2)), dma((WIDE, 2)), dma((WIDE + 3, 3)), dma((WIDE + 3, 3)),
             dma((2,)), dma((2,)), dma((5,)), dma((5,)), dma((2, 3)), dma((2, 3)),

time: 106 us -> 107 us (level)
    pallas_call x1, Pallas kernels: 104 us -> 105 us  [per_device(): pl.pallas_call(kernel, out_shape=jax.ShapeDtypeStruct((32, 2, 16, 32), F3...]
where the time goes in v7:
time: 107 us
  Pallas kernels  105 us (98%)
  local copies, waits for them, and re-layouts  1.87 us (2%)
    pallas_call x1, Pallas kernels, per_device(): pl.pallas_call(kernel, out_shape=jax.ShapeDtypeStruct((32, 2, 16, 32), F3...  105 us

profile of v7, /device:TPU:1, one launch (start us, length us, event | category | flops | bytes accessed | tf_op | source)
XLA Modules:
  0.0 107.0 jit_solution(10165033559469042720)
XLA Ops:
  0.0 105.1 %propagate.1 = f32[32,2,16,32]{3,2,1,0:T(8,128)} custom-call(bf16[1,2,512,512]{3,2,1,0:T(8,128)(2,1)} %x_ref.1), custom_call_target="tpu_custom_call" | custom-call | flops 3221225472 | bytes 4194304 | tf_op jit(solution)/shard_map/propagate/pallas_call | solution.py:506
  105.1 1.9 %copy.3 = f32[32,2,32,16]{2,3,1,0:T(8,128)} copy(f32[32,2,32,16]{2,3,1,0:T(8,128)} %bitcast.1) | data formatting | bytes 262144

commit v8 on v6

--- a/solution.py
+++ b/solution.py
@@ -374,8 +374,8 @@
                 final_out.at[order, d - 1], final_sem.at[order, d - 1], along_y(d),
             )
 
+    send(late.at[0], late.at[1], late_out.at[3], late_sem.at[3], opposite)
     send(late.at[0], late_shift, late_out.at[2], late_sem.at[2], cut(-16))
-    send(late.at[0], late.at[1], late_out.at[3], late_sem.at[3], opposite)
     spread_final(late.at[0], xh, 0)
     arrived(late.at[1], late_sem.at[3])
     spread_final(late.at[1], 1 - xh, 1)

time: 106 us -> 106 us (level)
  no operation moved by 1% of the time
where the time goes in v8:
time: 106 us; the launch traced here: 105 us
  Pallas kernels  104 us (98%)
  local copies, waits for them, and re-layouts  1.87 us (2%)
    pallas_call x1, Pallas kernels, per_device(): pl.pallas_call(kernel, out_shape=jax.ShapeDtypeStruct((32, 2, 16, 32), F3...  104 us

profile of v8, /device:TPU:1, one launch (start us, length us, event | category | flops | bytes accessed | tf_op | source)
XLA Modules:
  0.0 105.5 jit_solution(7720345790070456322)
XLA Ops:
  0.0 103.6 %propagate.1 = f32[32,2,16,32]{3,2,1,0:T(8,128)} custom-call(bf16[1,2,512,512]{3,2,1,0:T(8,128)(2,1)} %x_ref.1), custom_call_target="tpu_custom_call" | custom-call | flops 3221225472 | bytes 4194304 | tf_op jit(solution)/shard_map/propagate/pallas_call | solution.py:502
  103.6 1.9 %copy.3 = f32[32,2,32,16]{2,3,1,0:T(8,128)} copy(f32[32,2,32,16]{2,3,1,0:T(8,128)} %bitcast.1) | data formatting | bytes 262144
